TPU v7x, 256 devices: a whole 4x4x8 slice. The times are simulated.
256 devices in a mesh: tm: 8 (over y, x_hi), strip: 32 (over z, x_lo, core).
Axes of the slice: x: 4 (x_hi: 2, x_lo: 2; x = x_hi * 2 + x_lo), y: 4, z: 8, core: 2. Of those that a mesh axis runs over, the one named last changes fastest.
Arguments:
- video: bfloat16 [16, 128, 512, 256], P('tm', 'strip'), may hold values from -6 to 6
- gain_one: float32 [256], replicated, may hold values from 0.25 to 1.75
- conv_one: bfloat16 [3, 3, 256, 256], replicated, may hold values from -0.125 to 0.125
- gain_two: float32 [256], replicated, may hold values from 0.25 to 1.75
- conv_two: bfloat16 [3, 3, 256, 256], replicated, may hold values from -0.125 to 0.125
- gain_three: float32 [256], replicated, may hold values from 0.25 to 1.75
- time_kernel: bfloat16 [3, 256, 256], replicated, may hold values from -0.21875 to 0.21875
- gain_four: float32 [256], replicated, may hold values from 0.25 to 1.75
- query_weight: bfloat16 [256, 256], replicated
- key_weight: bfloat16 [256, 256], replicated
- value_weight: bfloat16 [256, 256], replicated, may hold values from -0.375 to 0.375
- out_weight: bfloat16 [256, 256], replicated, may hold values from -0.375 to 0.375
Outputs:
- encoded: bfloat16 [16, 128, 512, 256], P('tm', 'strip')
All inputs are finite; a program needn't handle non-finite values.
Results may differ from a plain program's by a relative error of at most 0.015.
Values may be sent and summed in bfloat16 or wider, within the bound.
No kernel may reach another device: no remote copies, remote signals or barrier semaphores. Data moves between devices by JAX's collectives and lax.ppermute only.
A program may use at most 128 MiB of HBM per device.

v0:
```python
import jax
import jax.numpy as jnp
from jax import lax
from jax.sharding import PartitionSpec as P


def padded_2(block, sides, width):
    for axis, dim in sides:
        count = lax.axis_size(axis)
        forward = [(i, i + 1) for i in range(count - 1)]
        backward = [(target, source) for source, target in forward]
        low = lax.ppermute(
            lax.slice_in_dim(block, block.shape[dim] - width, None, axis=dim), axis, forward
        )
        high = lax.ppermute(lax.slice_in_dim(block, 0, width, axis=dim), axis, backward)
        block = jnp.concatenate([low, block, high], axis=dim)
    return block


def normalize(values, gain):
    values = values.astype(jnp.float32)
    return values * lax.rsqrt(jnp.mean(values * values, axis=-1, keepdims=True) + 1e-06) * gain


def spatial(padded_rows, kernel):
    padded = jnp.pad(padded_rows, ((0, 0), (0, 0), (1, 1), (0, 0)))
    rows = padded.shape[1] - 2
    cols = padded.shape[2] - 2
    total = jnp.zeros((padded.shape[0], rows, cols, kernel.shape[3]), jnp.float32)
    for i in range(3):
        for j in range(3):
            piece = padded[:, i : i + rows, j : j + cols, :]
            total = total + jnp.dot(piece, kernel[i, j], preferred_element_type=jnp.float32)
    return total


def shards(
    video,
    gain_one,
    conv_one,
    gain_two,
    conv_two,
    gain_three,
    time_kernel,
    gain_four,
    query_weight,
    key_weight,
    value_weight,
    out_weight,
):
    first = jax.nn.silu(normalize(video, gain_one)).astype(jnp.bfloat16)
    first = padded_2(first, (("strip", 1),), 1)
    hidden = spatial(first, conv_one).astype(jnp.bfloat16)
    second = jax.nn.silu(normalize(hidden, gain_two)).astype(jnp.bfloat16)
    second = padded_2(second, (("strip", 1),), 1)
    mixed = (video.astype(jnp.float32) + spatial(second, conv_two)).astype(jnp.bfloat16)
    block = lax.all_to_all(mixed, "tm", split_axis=2, concat_axis=0, tiled=True)
    third = jax.nn.silu(normalize(block, gain_three)).astype(jnp.bfloat16)
    back_one = jnp.concatenate([third[:1], third[:-1]], axis=0)
    back_two = jnp.concatenate([third[:1], third[:1], third[:-2]], axis=0)
    change = jnp.dot(back_two, time_kernel[0], preferred_element_type=jnp.float32)
    change = change + jnp.dot(back_one, time_kernel[1], preferred_element_type=jnp.float32)
    change = change + jnp.dot(third, time_kernel[2], preferred_element_type=jnp.float32)
    timed = (block.astype(jnp.float32) + change).astype(jnp.bfloat16)
    fourth = normalize(timed, gain_four).astype(jnp.bfloat16)
    queries = jnp.dot(fourth, query_weight, preferred_element_type=jnp.float32).astype(jnp.bfloat16)
    keys = jnp.dot(fourth, key_weight, preferred_element_type=jnp.float32).astype(jnp.bfloat16)
    values = jnp.dot(fourth, value_weight, preferred_element_type=jnp.float32).astype(jnp.bfloat16)
    frames = block.shape[0]
    causal = jnp.arange(frames)[:, None] >= jnp.arange(frames)[None, :]
    scores = jnp.einsum("trwc,srwc->rwts", queries, keys, preferred_element_type=jnp.float32)
    scores = scores / jnp.sqrt(jnp.float32(queries.shape[-1]))
    scores = jnp.where(causal[None, None], scores, -1e30)
    weights = jax.nn.softmax(scores, axis=-1).astype(jnp.bfloat16)
    attended = jnp.einsum(
        "rwts,srwc->trwc", weights, values, preferred_element_type=jnp.float32
    ).astype(jnp.bfloat16)
    final = timed.astype(jnp.float32) + jnp.dot(
        attended, out_weight, preferred_element_type=jnp.float32
    )
    final = final.astype(jnp.bfloat16)
    return lax.all_to_all(final, "tm", split_axis=0, concat_axis=2, tiled=True)


def solution(mesh):
    placed = (P("tm", "strip", None, None), P(), P(), P(), P(), P(), P(), P(), P(), P(), P(), P())
    return jax.shard_map(
        shards, mesh=mesh, in_specs=placed, out_specs=P("tm", "strip", None, None), check_vma=False
    )
```

profile of v0, /device:TPU:160, one launch (start us, length us, event | category | flops | bytes accessed | tf_op | source)
XLA Modules:
  0.0 200.1 jit_solution(8029979781666983617)
XLA Ops:
  0.0 2.4 %fusion.10 = f32[2,4,512]{2,1,0:T(4,128)S(1)} fusion(bf16[2,4,512,256]{3,2,1,0:T(8,128)(2,1)} %param.12), kind=kLoop, calls=%fused_computation.20 | loop fusion | flops 3141632 | bytes 2113536 | tf_op jit(solution)/shard_map/reduce_sum | solution.py:22
  2.4 2.2 %fusion.17 = bf16[2,4,512,256]{3,2,1,0:T(8,128)(2,1)S(1)} fusion(bf16[2,4,512,256]{3,2,1,0:T(8,128)(2,1)S(1)} %copy-done.1, f32[256]{0:T(256)} %param.13, f32[2,4,512]{2,1,0:T(4,128)S(1)} %add_rsqrt_fusion.3), kind=kLoop, calls=%fused_computation.27 | loop fusion | flops 8388608 | bytes 4211712 | tf_op jit(solution)/shard_map/convert_element_type | solution.py:51
  6.6 4.5 %collective-permute-start.1 = (bf16[2,1,512,256]{3,2,1,0:T(8,128)(2,1)S(1)}, bf16[2,1,512,256]{3,2,1,0:T(8,128)(2,1)S(1)}, u32[]{:S(2)}, u32[]{:S(2)}) collective-permute-start(bf16[2,1,512,256]{3,2,1,0:T(8,128)(2,1)S(1)} %get-tuple-element.8), channel_id=1, source_target_pairs={{1,0},{2,1},{3,2},{4,3},{5,4},{6,5},{7,6},{8,7},{9,8},{10,9},{11,1... | collective-permute-start | bytes 1572872 | tf_op jit(solution)/shard_map/ppermute | solution.py:15
  11.1 2.7 %fusion.125 = f32[2,4,512,256]{3,2,1,0:T(8,128)} fusion(bf16[2,4,512,256]{3,2,1,0:T(8,128)(2,1)S(1)} %fusion.17, bf16[3,3,256,256]{3,2,1,0:T(8,128)(2,1)S(1)} %copy-done.4), kind=kOutput, calls=%fused_computation.139 | convolution fusion | flops 536870912 | bytes 6422528 | tf_op jit(solution)/shard_map/dot_general | solution.py:33
  13.8 2.4 %collective-permute-done = bf16[2,1,512,256]{3,2,1,0:T(8,128)(2,1)S(1)} collective-permute-done((bf16[2,1,512,256]{3,2,1,0:T(8,128)(2,1)S(1)}, bf16[2,1,512,256]{3,2,1,0:T(8,128)(2,1)S(1)}, u32[]{:S(2)}, u32[]{:S(2)}) %collective-permute-start) | collective-permute-done | bytes 524320 | tf_op jit(solution)/shard_map/ppermute | solution.py:12
  18.9 2.7 %fusion.71 = f32[2,4,512,256]{3,2,1,0:T(8,128)} fusion(bf16[2,6,514,256]{3,2,1,0:T(8,128)(2,1)S(1)} %fusion.30, bf16[3,3,256,256]{3,2,1,0:T(8,128)(2,1)S(1)} %copy-done.4), kind=kOutput, calls=%fused_computation.87 | convolution fusion | flops 536870912 | bytes 6422528 | tf_op jit(solution)/shard_map/dot_general | solution.py:33
  21.6 2.7 %fusion.73 = f32[2,4,512,256]{3,2,1,0:T(8,128)} fusion(bf16[2,6,514,256]{3,2,1,0:T(8,128)(2,1)S(1)} %fusion.30, bf16[3,3,256,256]{3,2,1,0:T(8,128)(2,1)S(1)} %copy-done.4), kind=kOutput, calls=%fused_computation.89 | convolution fusion | flops 536870912 | bytes 6422528 | tf_op jit(solution)/shard_map/dot_general | solution.py:33
  24.3 2.6 %fusion.75 = f32[2,4,512,256]{3,2,1,0:T(8,128)} fusion(bf16[2,6,514,256]{3,2,1,0:T(8,128)(2,1)S(1)} %fusion.30, bf16[3,3,256,256]{3,2,1,0:T(8,128)(2,1)S(1)} %copy-done.4), kind=kOutput, calls=%fused_computation.91 | convolution fusion | flops 536870912 | bytes 6422528 | tf_op jit(solution)/shard_map/dot_general | solution.py:33
  26.9 2.7 %fusion.77 = f32[2,4,512,256]{3,2,1,0:T(8,128)} fusion(bf16[2,6,514,256]{3,2,1,0:T(8,128)(2,1)S(1)} %fusion.30, bf16[3,3,256,256]{3,2,1,0:T(8,128)(2,1)S(1)} %copy-done.4), kind=kOutput, calls=%fused_computation.93 | convolution fusion | flops 536870912 | bytes 6422528 | tf_op jit(solution)/shard_map/dot_general | solution.py:33
  29.6 2.7 %fusion.79 = f32[2,4,512,256]{3,2,1,0:T(8,128)} fusion(bf16[2,6,514,256]{3,2,1,0:T(8,128)(2,1)S(1)} %fusion.30, bf16[3,3,256,256]{3,2,1,0:T(8,128)(2,1)S(1)} %copy-done.4), kind=kOutput, calls=%fused_computation.95 | convolution fusion | flops 536870912 | bytes 6422528 | tf_op jit(solution)/shard_map/dot_general | solution.py:33
  32.3 2.6 %fusion.31 = f32[2,4,512,256]{3,2,1,0:T(8,128)} fusion(bf16[2,4,512,256]{3,2,1,0:T(8,128)(2,1)S(1)} %fusion.17, bf16[2,1,512,256]{3,2,1,0:T(8,128)(2,1)S(1)} %collective-permute-done, bf16[3,3,256,256]{3,2,1,0:T(8,128)(2,1)S(1)} %copy-done.4), kind=kOutput, calls=%fused_computation.53 | convolution fusion | flops 542113792 | bytes 6946816 | tf_op jit(solution)/shard_map/dot_general | solution.py:33
  34.9 2.6 %fusion.35 = f32[2,4,512,256]{3,2,1,0:T(8,128)} fusion(bf16[2,1,512,256]{3,2,1,0:T(8,128)(2,1)S(1)} %collective-permute-done.1, bf16[2,4,512,256]{3,2,1,0:T(8,128)(2,1)S(1)} %fusion.17, bf16[3,3,256,256]{3,2,1,0:T(8,128)(2,1)S(1)} %copy-done.4), kind=kOutput, calls=%fused_computation.57 | convolution fusion | flops 542113792 | bytes 6946816 | tf_op jit(solution)/shard_map/dot_general | solution.py:33
  37.6 13.1 %fusion.2 = (f32[2,4,512]{2,1,0:T(4,128)S(1)}, bf16[2,4,512,256]{3,2,1,0:T(8,128)(2,1)}) fusion(bf16[3,3,256,256]{3,2,1,0:T(8,128)(2,1)S(1)} %copy-done.4, bf16[2,6,514,256]{3,2,1,0:T(8,128)(2,1)S(1)} %fusion.30, f32[2,4,512,256]{3,2,1,0:T(8,128)} %fusion.35, f32[2,4,512,256]{3,2,1,0:T(8,128)} %fusion.71, f32[2,4,512,256]{3,2,1,0:T(8,128)} %fusion.73, ...), kind=kOutput, calls=%fused_computation.12 | convolution fusion | flops 549449728 | bytes 37896192 | tf_op jit(solution)/shard_map/dot_general | solution.py:33
  50.7 2.7 %fusion.9 = bf16[2,4,512,256]{3,2,1,0:T(8,128)(2,1)S(1)} fusion(bf16[2,4,512,256]{3,2,1,0:T(8,128)(2,1)} %get-tuple-element.10, f32[256]{0:T(256)S(1)} %copy-done.9, f32[2,4,512]{2,1,0:T(4,128)S(1)} %add_rsqrt_fusion.2), kind=kLoop, calls=%fused_computation.19 | loop fusion | flops 8388608 | bytes 4211712 | tf_op jit(solution)/shard_map/convert_element_type | solution.py:54
  53.5 5.5 %collective-permute-start.2 = (bf16[2,1,512,256]{3,2,1,0:T(8,128)(2,1)S(1)}, bf16[2,1,512,256]{3,2,1,0:T(8,128)(2,1)S(1)}, u32[]{:S(2)}, u32[]{:S(2)}) collective-permute-start(bf16[2,1,512,256]{3,2,1,0:T(8,128)(2,1)S(1)} %get-tuple-element.5), channel_id=1, source_target_pairs={{0,1},{1,2},{2,3},{3,4},{4,5},{5,6},{6,7},{7,8},{8,9},{9,10},{10,1... | collective-permute-start | bytes 1572872 | tf_op jit(solution)/shard_map/ppermute | solution.py:12
  59.0 2.1 %collective-permute-start.3 = (bf16[2,1,512,256]{3,2,1,0:T(8,128)(2,1)S(1)}, bf16[2,1,512,256]{3,2,1,0:T(8,128)(2,1)S(1)}, u32[]{:S(2)}, u32[]{:S(2)}) collective-permute-start(bf16[2,1,512,256]{3,2,1,0:T(8,128)(2,1)S(1)} %get-tuple-element.6), channel_id=1, source_target_pairs={{1,0},{2,1},{3,2},{4,3},{5,4},{6,5},{7,6},{8,7},{9,8},{10,9},{11,1... | collective-permute-start | bytes 1572872 | tf_op jit(solution)/shard_map/ppermute | solution.py:15
  61.2 2.6 %fusion.115 = f32[2,4,512,256]{3,2,1,0:T(8,128)} fusion(bf16[2,4,512,256]{3,2,1,0:T(8,128)(2,1)S(1)} %fusion.9, bf16[3,3,256,256]{3,2,1,0:T(8,128)(2,1)S(1)} %copy-done.5), kind=kOutput, calls=%fused_computation.129 | convolution fusion | flops 536870912 | bytes 6422528 | tf_op jit(solution)/shard_map/dot_general | solution.py:33
  65.1 2.6 %collective-permute-done.3 = bf16[2,1,512,256]{3,2,1,0:T(8,128)(2,1)S(1)} collective-permute-done((bf16[2,1,512,256]{3,2,1,0:T(8,128)(2,1)S(1)}, bf16[2,1,512,256]{3,2,1,0:T(8,128)(2,1)S(1)}, u32[]{:S(2)}, u32[]{:S(2)}) %collective-permute-start.3) | collective-permute-done | bytes 524320 | tf_op jit(solution)/shard_map/ppermute | solution.py:15
  68.7 2.7 %fusion.57 = f32[2,4,512,256]{3,2,1,0:T(8,128)} fusion(bf16[2,6,514,256]{3,2,1,0:T(8,128)(2,1)S(1)} %select_maximum_fusion, bf16[3,3,256,256]{3,2,1,0:T(8,128)(2,1)S(1)} %copy-done.5), kind=kOutput, calls=%fused_computation.75 | convolution fusion | flops 536870912 | bytes 6422528 | tf_op jit(solution)/shard_map/dot_general | solution.py:33
  71.4 2.7 %fusion.59 = f32[2,4,512,256]{3,2,1,0:T(8,128)} fusion(bf16[2,6,514,256]{3,2,1,0:T(8,128)(2,1)S(1)} %select_maximum_fusion, bf16[3,3,256,256]{3,2,1,0:T(8,128)(2,1)S(1)} %copy-done.5), kind=kOutput, calls=%fused_computation.77 | convolution fusion | flops 536870912 | bytes 6422528 | tf_op jit(solution)/shard_map/dot_general | solution.py:33
  74.1 2.6 %fusion.61 = f32[2,4,512,256]{3,2,1,0:T(8,128)} fusion(bf16[2,6,514,256]{3,2,1,0:T(8,128)(2,1)S(1)} %select_maximum_fusion, bf16[3,3,256,256]{3,2,1,0:T(8,128)(2,1)S(1)} %copy-done.5), kind=kOutput, calls=%fused_computation.79 | convolution fusion | flops 536870912 | bytes 6422528 | tf_op jit(solution)/shard_map/dot_general | solution.py:33
  76.7 2.7 %fusion.63 = f32[2,4,512,256]{3,2,1,0:T(8,128)} fusion(bf16[2,6,514,256]{3,2,1,0:T(8,128)(2,1)S(1)} %select_maximum_fusion, bf16[3,3,256,256]{3,2,1,0:T(8,128)(2,1)S(1)} %copy-done.5), kind=kOutput, calls=%fused_computation.81 | convolution fusion | flops 536870912 | bytes 6422528 | tf_op jit(solution)/shard_map/dot_general | solution.py:33
  79.5 2.7 %fusion.65 = f32[2,4,512,256]{3,2,1,0:T(8,128)} fusion(bf16[2,6,514,256]{3,2,1,0:T(8,128)(2,1)S(1)} %select_maximum_fusion, bf16[3,3,256,256]{3,2,1,0:T(8,128)(2,1)S(1)} %copy-done.5), kind=kOutput, calls=%fused_computation.83 | convolution fusion | flops 536870912 | bytes 6422528 | tf_op jit(solution)/shard_map/dot_general | solution.py:33
  82.1 2.6 %fusion.39 = f32[2,4,512,256]{3,2,1,0:T(8,128)} fusion(bf16[2,4,512,256]{3,2,1,0:T(8,128)(2,1)S(1)} %fusion.9, bf16[2,1,512,256]{3,2,1,0:T(8,128)(2,1)S(1)} %collective-permute-done.2, bf16[3,3,256,256]{3,2,1,0:T(8,128)(2,1)S(1)} %copy-done.5), kind=kOutput, calls=%fused_computation.61 | convolution fusion | flops 542113792 | bytes 6946816 | tf_op jit(solution)/shard_map/dot_general | solution.py:33
  84.8 2.6 %fusion.43 = f32[2,4,512,256]{3,2,1,0:T(8,128)} fusion(bf16[2,1,512,256]{3,2,1,0:T(8,128)(2,1)S(1)} %collective-permute-done.3, bf16[2,4,512,256]{3,2,1,0:T(8,128)(2,1)S(1)} %fusion.9, bf16[3,3,256,256]{3,2,1,0:T(8,128)(2,1)S(1)} %copy-done.5), kind=kOutput, calls=%fused_computation.65 | convolution fusion | flops 542113792 | bytes 6946816 | tf_op jit(solution)/shard_map/dot_general | solution.py:33
  87.4 11.8 %fusion.18 = bf16[2,4,512,256]{3,2,1,0:T(8,128)(2,1)S(1)} fusion(bf16[2,4,512,256]{3,2,1,0:T(8,128)(2,1)S(1)} %copy-done.1, f32[2,4,512,256]{3,2,1,0:T(8,128)} %fusion.43, f32[2,4,512,256]{3,2,1,0:T(8,128)} %fusion.57, f32[2,4,512,256]{3,2,1,0:T(8,128)} %fusion.59, f32[2,4,512,256]{3,2,1,0:T(8,128)} %fusion.115, f32[2,4,512,256]{3,2,1,0:T(8,128)} %fusion.61, ...), kind=kOutput, calls=%fused_computation.28 | convolution fusion | flops 548405248 | bytes 39976960 | tf_op jit(solution)/shard_map/dot_general | solution.py:33
  99.2 2.9 %copy.17 = bf16[2,4,512,256]{3,1,0,2:T(4,128)(2,1)} copy(bf16[2,4,512,256]{3,2,1,0:T(8,128)(2,1)S(1)} %fusion.18) | data formatting | bytes 4194304 | tf_op jit(solution)/shard_map/convert_element_type | solution.py:56
  102.1 6.9 %all-to-all-start = ((bf16[2,4,512,256]{3,1,0,2:T(4,128)(2,1)}), bf16[2,4,512,256]{3,1,0,2:T(4,128)(2,1)S(1)}, u32[]{:S(2)}, u32[]{:S(2)}) async-start(bf16[2,4,512,256]{3,1,0,2:T(4,128)(2,1)} %copy.17), calls=%async_computation | async-start | bytes 4194304 | tf_op jit(solution)/shard_map/all_to_all | solution.py:57
  109.1 27.4 %all-to-all-done = bf16[2,4,512,256]{3,1,0,2:T(4,128)(2,1)S(1)} async-done(((bf16[2,4,512,256]{3,1,0,2:T(4,128)(2,1)}), bf16[2,4,512,256]{3,1,0,2:T(4,128)(2,1)S(1)}, u32[]{:S(2)}, u32[]{:S(2)}) %all-to-all-start) | async-done | bytes 2097184 | tf_op jit(solution)/shard_map/all_to_all | solution.py:57
  152.3 7.4 %fusion.162 = (f32[4,64,16]{2,1,0:T(8,128)S(1)}, f32[4,64,16,16]{2,3,1,0:T(8,128)}) fusion(pred[16,16]{0,1:T(8,128)(4,1)S(1)} %iota_compare_fusion.2, bf16[16,4,64,256]{3,2,1,0:T(8,128)(2,1)} %copy-done.3, bf16[256,256]{1,0:T(8,128)(2,1)S(1)} %copy-done.11, bf16[256,256]{1,0:T(8,128)(2,1)S(1)} %copy-done.12), kind=kOutput, calls=%fused_computation.181 | convolution fusion | flops 1109655552 | bytes 2638080 | tf_op jit(solution)/shard_map/sub | solution.py:74
  159.7 3.7 %fusion.84 = bf16[4,64,256,16]{2,3,1,0:T(8,128)(2,1)S(1)} fusion(bf16[16,4,64,256]{3,2,1,0:T(8,128)(2,1)} %convolution_convert_fusion, f32[4,64,16,16]{2,3,1,0:T(8,128)} %get-tuple-element.12, f32[4,64,16]{2,1,0:T(8,128)S(1)} %get-tuple-element.11), kind=kOutput, calls=%fused_computation.100 | convolution fusion | flops 33685504 | bytes 4472832 | tf_op jit(solution)/shard_map/rwts,srwc->trwc/dot_general | solution.py:75
  165.0 33.6 %all_to_all.27 = bf16[16,4,64,256]{3,2,1,0:T(8,128)(2,1)S(1)} all-to-all(bf16[16,4,64,256]{3,2,1,0:T(8,128)(2,1)S(1)} %fusion.22), channel_id=1, replica_groups=mesh['tm'=8,'strip'=32] {'tm'}, dimensions={0} | all-to-all | bytes 4194304 | tf_op jit(solution)/shard_map/all_to_all | solution.py:82
  (55 shorter events, 25.9 us)
Async XLA Ops:
  0.0 150.3 %copy-start = (bf16[256,256]{1,0:T(8,128)(2,1)S(1)}, bf16[256,256]{1,0:T(8,128)(2,1)}, u32[]{:S(2)}) copy-start(bf16[256,256]{1,0:T(8,128)(2,1)} %param.22) | copy-start | bytes 393220
  0.0 2.4 %copy-start.1 = (bf16[2,4,512,256]{3,2,1,0:T(8,128)(2,1)S(1)}, bf16[2,4,512,256]{3,2,1,0:T(8,128)(2,1)}, u32[]{:S(2)}) copy-start(bf16[2,4,512,256]{3,2,1,0:T(8,128)(2,1)} %param.12) | copy-start | bytes 6291460
  2.4 8.8 %copy-start.4 = (bf16[3,3,256,256]{3,2,1,0:T(8,128)(2,1)S(1)}, bf16[3,3,256,256]{3,2,1,0:T(8,128)(2,1)}, u32[]{:S(2)}) copy-start(bf16[3,3,256,256]{3,2,1,0:T(8,128)(2,1)} %param.14) | copy-start | bytes 3538948
  4.7 11.5 %collective-permute-start = (bf16[2,1,512,256]{3,2,1,0:T(8,128)(2,1)S(1)}, bf16[2,1,512,256]{3,2,1,0:T(8,128)(2,1)S(1)}, u32[]{:S(2)}, u32[]{:S(2)}) collective-permute-start(bf16[2,1,512,256]{3,2,1,0:T(8,128)(2,1)S(1)} %get-tuple-element.7), channel_id=1, source_target_pairs={{0,1},{1,2},{2,3},{3,4},{4,5},{5,6},{6,7},{7,8},{8,9},{9,10},{10,1... | collective-permute-start | bytes 1572872 | tf_op jit(solution)/shard_map/ppermute | solution.py:12
  6.6 11.3 %collective-permute-start.1 = (bf16[2,1,512,256]{3,2,1,0:T(8,128)(2,1)S(1)}, bf16[2,1,512,256]{3,2,1,0:T(8,128)(2,1)S(1)}, u32[]{:S(2)}, u32[]{:S(2)}) collective-permute-start(bf16[2,1,512,256]{3,2,1,0:T(8,128)(2,1)S(1)} %get-tuple-element.8), channel_id=1, source_target_pairs={{1,0},{2,1},{3,2},{4,3},{5,4},{6,5},{7,6},{8,7},{9,8},{10,9},{11,1... | collective-permute-start | bytes 1572872 | tf_op jit(solution)/shard_map/ppermute | solution.py:15
  37.6 13.1 %copy-start.9 = (f32[256]{0:T(256)S(1)}, f32[256]{0:T(256)}, u32[]{:S(2)}) copy-start(f32[256]{0:T(256)} %param.15) | copy-start | bytes 3076
  50.7 10.5 %copy-start.5 = (bf16[3,3,256,256]{3,2,1,0:T(8,128)(2,1)S(1)}, bf16[3,3,256,256]{3,2,1,0:T(8,128)(2,1)}, u32[]{:S(2)}) copy-start(bf16[3,3,256,256]{3,2,1,0:T(8,128)(2,1)} %param.16) | copy-start | bytes 3538948
  53.5 11.6 %collective-permute-start.2 = (bf16[2,1,512,256]{3,2,1,0:T(8,128)(2,1)S(1)}, bf16[2,1,512,256]{3,2,1,0:T(8,128)(2,1)S(1)}, u32[]{:S(2)}, u32[]{:S(2)}) collective-permute-start(bf16[2,1,512,256]{3,2,1,0:T(8,128)(2,1)S(1)} %get-tuple-element.5), channel_id=1, source_target_pairs={{0,1},{1,2},{2,3},{3,4},{4,5},{5,6},{6,7},{7,8},{8,9},{9,10},{10,1... | collective-permute-start | bytes 1572872 | tf_op jit(solution)/shard_map/ppermute | solution.py:12
  59.0 8.7 %collective-permute-start.3 = (bf16[2,1,512,256]{3,2,1,0:T(8,128)(2,1)S(1)}, bf16[2,1,512,256]{3,2,1,0:T(8,128)(2,1)S(1)}, u32[]{:S(2)}, u32[]{:S(2)}) collective-permute-start(bf16[2,1,512,256]{3,2,1,0:T(8,128)(2,1)S(1)} %get-tuple-element.6), channel_id=1, source_target_pairs={{1,0},{2,1},{3,2},{4,3},{5,4},{6,5},{7,6},{8,7},{9,8},{10,9},{11,1... | collective-permute-start | bytes 1572872 | tf_op jit(solution)/shard_map/ppermute | solution.py:15
  102.1 34.3 %all-to-all-start = ((bf16[2,4,512,256]{3,1,0,2:T(4,128)(2,1)}), bf16[2,4,512,256]{3,1,0,2:T(4,128)(2,1)S(1)}, u32[]{:S(2)}, u32[]{:S(2)}) async-start(bf16[2,4,512,256]{3,1,0,2:T(4,128)(2,1)} %copy.17), calls=%async_computation | async-start | bytes 4194304 | tf_op jit(solution)/shard_map/all_to_all | solution.py:57
  138.3 0.7 copy-start.8
  140.6 1.3 copy-start.2
  141.9 1.7 copy-start.6
  143.6 1.5 slice-start
  145.8 2.1 %copy-start.10 = (f32[256]{0:T(256)S(1)}, f32[256]{0:T(256)}, u32[]{:S(2)}) copy-start(f32[256]{0:T(256)} %param.19) | copy-start | bytes 3076
  148.9 1.3 copy-start.3
  150.3 2.0 %copy-start.11 = (bf16[256,256]{1,0:T(8,128)(2,1)S(1)}, bf16[256,256]{1,0:T(8,128)(2,1)}, u32[]{:S(2)}) copy-start(bf16[256,256]{1,0:T(8,128)(2,1)} %param.21) | copy-start | bytes 393220
  150.3 2.0 %copy-start.12 = (bf16[256,256]{1,0:T(8,128)(2,1)S(1)}, bf16[256,256]{1,0:T(8,128)(2,1)}, u32[]{:S(2)}) copy-start(bf16[256,256]{1,0:T(8,128)(2,1)} %param.20) | copy-start | bytes 393220
  159.7 3.7 %copy-start.7 = (bf16[256,256]{1,0:T(8,128)(2,1)S(1)}, bf16[256,256]{1,0:T(8,128)(2,1)}, u32[]{:S(2)}) copy-start(bf16[256,256]{1,0:T(8,128)(2,1)} %param.23) | copy-start | bytes 393220
where the time goes:
time: 202 us; the launch traced here: 200 us
  matrix products  85.2 us (42%)
  waiting for transfers between devices  35.4 us (18%)
  blocking collectives  33.6 us (17%)
  starting transfers between devices  21 us (10%)
  other arithmetic  16 us (8%)
  local copies, waits for them, and re-layouts  8.64 us (4%)
    dot_general x18, matrix products, spatial(): jnp.dot(piece, kernel[i, j], preferred_element_type=jnp.float32)  67.5 us
    all_to_all x1, blocking collectives, shards(): return lax.all_to_all(final, 'tm', split_axis=0, concat_axis=2, tiled=True)  33.6 us
    all_to_all x1, waiting for transfers between devices, shards(): block = lax.all_to_all(mixed, 'tm', split_axis=2, concat_axis=0, tiled=True)  27.4 us
    ppermute x2, starting transfers between devices, padded_2(): lax.ppermute(lax.slice_in_dim(block, block.shape[dim] - width, None, axis...  7.46 us
    sub x1, matrix products, shards(): weights = jax.nn.softmax(scores, axis=-1).astype(jnp.bfloat16)  7.42 us
    all_to_all x1, starting transfers between devices, shards(): block = lax.all_to_all(mixed, 'tm', split_axis=2, concat_axis=0, tiled=True)  6.93 us
    ppermute x2, starting transfers between devices, padded_2(): lax.ppermute(lax.slice_in_dim(block, 0, width, axis=dim), axis, backward)  6.64 us
    ppermute x2, waiting for transfers between devices, padded_2(): lax.ppermute(lax.slice_in_dim(block, 0, width, axis=dim), axis, backward)  4.26 us
  transfers between devices with their start and end apart: 5, of which 5 were waited for; matrix products, arithmetic and copies ran while one was open for 3% of the time, Pallas kernels for 0%

commit v1 on v0

v1 whole, which is shorter than its diff:
```python
import functools

import jax
import jax.numpy as jnp
from jax import lax
from jax.experimental import pallas as pl
from jax.experimental.pallas import tpu as pltpu
from jax.sharding import PartitionSpec as P

BF16 = jnp.bfloat16
F32 = jnp.float32
EDGE = 16
EPS = 1e-06


def scaled(values, gain):
    mean = jnp.mean(values * values, axis=-1, keepdims=True)
    return values * lax.rsqrt(mean + EPS) * gain


def silu_from_half(half):
    return half + half * jnp.tanh(half)


def put_shifted(dst, row, values):
    width, chans = values.shape
    index = lax.broadcasted_iota(jnp.int32, (width, 1), 0)
    before = jnp.where(index == 0, 0.0, pltpu.roll(values, 1, 0))
    after = jnp.where(index == width - 1, 0.0, pltpu.roll(values, width - 1, 0))
    dst[row, :, 0:chans] = before.astype(BF16)
    dst[row, :, chans : 2 * chans] = values.astype(BF16)
    dst[row, :, 2 * chans : 3 * chans] = after.astype(BF16)


def conv_body(plan, flags, video, *refs):
    (window, keep, parts, owners, rows) = plan
    halos, (gain_one, conv_one, gain_two, conv_two, out, s_one, s_two) = refs[:-7], refs[-7:]
    start, stop = window
    width = stop - start
    half_one = gain_one[...] * 0.5
    half_two = gain_two[...] * 0.5
    chans = gain_one.shape[-1]

    def halo_row(side, row):
        pieces = []
        for number, (low, high) in enumerate(parts):
            a, b = max(low, start), min(high, stop)
            if a < b:
                pieces.append(halos[2 * number + side][0, row, a - low : b - low, :])
        return pieces[0] if len(pieces) == 1 else jnp.concatenate(pieces, axis=0)

    for row in range(rows + 4):
        if row < 2:
            raw = halo_row(0, row)
        elif row < rows + 2:
            raw = video[0, row - 2, start:stop, :]
        else:
            raw = halo_row(1, row - rows - 2)
        put_shifted(s_one, row, silu_from_half(scaled(raw.astype(F32), half_one)))

    def product(source, weights, row):
        lhs = jnp.concatenate([source[row + i] for i in range(3)], axis=-1)
        return jnp.dot(lhs, weights[...], preferred_element_type=F32)

    for row in range(rows + 2):
        hidden = product(s_one, conv_one, row)
        second = silu_from_half(scaled(hidden, half_two))
        if row == 0:
            second = second * flags[0]
        if row == rows + 1:
            second = second * flags[1]
        put_shifted(s_two, row, second)

    low, high = keep[0] - start, keep[1] - start
    for row in range(rows):
        change = product(s_two, conv_two, row)[low:high]
        base = video[0, row, keep[0] : keep[1], :].astype(F32)
        mixed = (base + change).astype(BF16)
        out[:, 0, row] = mixed.reshape(owners, (high - low) // owners, chans)


def conv_chunk(video, flags, halos, parts, window, keep, owners, weights):
    frames, rows, cols, chans = video.shape
    gain_one, conv_one, gain_two, conv_two = weights
    width = window[1] - window[0]
    own = (keep[1] - keep[0]) // owners
    plan = (window, keep, parts, owners, rows)
    whole = lambda shape: pl.BlockSpec(shape, lambda f: (0,) * len(shape))
    halo_specs = [
        pl.BlockSpec((1,) + h.shape[1:], lambda f: (f, 0, 0, 0)) for h in halos
    ]
    flops = 2 * frames * (2 * rows + 2) * width * 9 * chans * chans
    return pl.pallas_call(
        functools.partial(conv_body, plan),
        grid=(frames,),
        in_specs=[
            pl.BlockSpec(memory_space=pltpu.SMEM),
            pl.BlockSpec((1, rows, cols, chans), lambda f: (f, 0, 0, 0)),
            *halo_specs,
            whole((1, chans)),
            whole((9 * chans, chans)),
            whole((1, chans)),
            whole((9 * chans, chans)),
        ],
        out_specs=pl.BlockSpec((owners, 1, rows, own, chans), lambda f: (0, f, 0, 0, 0)),
        out_shape=jax.ShapeDtypeStruct((owners, frames, rows, own, chans), BF16),
        scratch_shapes=[
            pltpu.VMEM((rows + 4, width, 3 * chans), BF16),
            pltpu.VMEM((rows + 2, width, 3 * chans), BF16),
        ],
        compiler_params=pltpu.CompilerParams(vmem_limit_bytes=40 * 1024 * 1024),
        cost_estimate=pl.CostEstimate(flops=flops, bytes_accessed=8 * 1024 * 1024, transcendentals=0),
        name="convs",
    )(flags, video, *halos, gain_one, conv_one, gain_two, conv_two)


def attend_body(group, x_ref, gain_three, kernel, gain_four, wq, wk, wv, wo, out_ref):
    frames, pixels, chans = x_ref.shape
    count = frames * pixels
    half_three = gain_three[...] * 0.5
    x = x_ref[...].reshape(count, chans).astype(F32)
    third = silu_from_half(scaled(x, half_three)).astype(BF16).reshape(frames, pixels, chans)
    one = jnp.concatenate([third[:1], third[:-1]], axis=0)
    two = jnp.concatenate([third[:1], third[:1], third[:-2]], axis=0)
    taps = jnp.concatenate([two, one, third], axis=-1).reshape(count, 3 * chans)
    timed = x + jnp.dot(taps, kernel[...], preferred_element_type=F32)
    fourth = scaled(timed, gain_four[...]).astype(BF16)
    project = lambda w: jnp.dot(fourth, w[...], preferred_element_type=F32)
    scale = 1.0 / float(chans) ** 0.5
    queries = (project(wq) * scale).astype(BF16).reshape(frames, pixels, chans)
    keys = project(wk).astype(BF16).reshape(frames, pixels, chans)
    values = project(wv).astype(BF16).reshape(frames, pixels, chans)
    size = frames * group
    down = lax.broadcasted_iota(jnp.int32, (size, size), 0)
    along = lax.broadcasted_iota(jnp.int32, (size, size), 1)
    allowed = (down % group == along % group) & (down >= along)
    pieces = []
    for g in range(pixels // group):
        cut = lambda v: v[:, g * group : (g + 1) * group].reshape(size, chans)
        scores = lax.dot_general(
            cut(queries), cut(keys), (((1,), (1,)), ((), ())), preferred_element_type=F32
        )
        scores = jnp.where(allowed, scores, -1e30)
        top = jnp.max(scores, axis=-1, keepdims=True)
        weights = jnp.exp(scores - top)
        total = jnp.sum(weights, axis=-1, keepdims=True)
        weights = (weights * (1.0 / total)).astype(BF16)
        attended = jnp.dot(weights, cut(values), preferred_element_type=F32)
        pieces.append(attended.astype(BF16).reshape(frames, group, chans))
    attended = pieces[0] if len(pieces) == 1 else jnp.concatenate(pieces, axis=1)
    final = timed + jnp.dot(
        attended.reshape(count, chans), wo[...], preferred_element_type=F32
    )
    out_ref[...] = final.astype(BF16).reshape(frames, pixels, chans)


def attend_chunk(x, weights, tile, group):
    frames, pixels, chans = x.shape
    tile = min(tile, pixels)
    whole = lambda a: pl.BlockSpec(a.shape, lambda p: (0,) * a.ndim)
    spec = pl.BlockSpec((frames, tile, chans), lambda p: (0, p, 0))
    return pl.pallas_call(
        functools.partial(attend_body, group),
        grid=(pixels // tile,),
        in_specs=[spec] + [whole(w) for w in weights],
        out_specs=spec,
        out_shape=jax.ShapeDtypeStruct(x.shape, BF16),
        compiler_params=pltpu.CompilerParams(vmem_limit_bytes=40 * 1024 * 1024),
        cost_estimate=pl.CostEstimate(
            flops=2 * frames * pixels * chans * chans * 9,
            bytes_accessed=4 * 1024 * 1024,
            transcendentals=0,
        ),
        name="attend",
    )(x, *weights)


def shards(
    video,
    gain_one,
    conv_one,
    gain_two,
    conv_two,
    gain_three,
    time_kernel,
    gain_four,
    query_weight,
    key_weight,
    value_weight,
    out_weight,
):
    frames, rows, cols, chans = video.shape
    owners = lax.axis_size("tm")
    strips = lax.axis_size("strip")
    strip = lax.axis_index("strip")
    chunks = 2
    step = cols // chunks
    forward = [(i, i + 1) for i in range(strips - 1)]
    backward = [(i + 1, i) for i in range(strips - 1)]
    flags = jnp.stack([strip > 0, strip < strips - 1]).astype(F32)
    row = lambda gain: gain.reshape(1, chans)
    flat = lambda w: w.reshape(-1, chans)
    conv_weights = (row(gain_one), flat(conv_one), row(gain_two), flat(conv_two))
    attend_weights = (
        row(gain_three), flat(time_kernel), row(gain_four),
        query_weight, key_weight, value_weight, out_weight,
    )

    edges = [0] + [min(step * (c + 1) + EDGE, cols) for c in range(chunks)]
    parts = [(edges[c], edges[c + 1]) for c in range(chunks)]
    halos = []
    for low, high in parts:
        halos.append(lax.ppermute(video[:, rows - 2 :, low:high], "strip", forward))
        halos.append(lax.ppermute(video[:, :2, low:high], "strip", backward))

    outs = []
    for c in range(chunks):
        keep = (c * step, (c + 1) * step)
        window = (max(keep[0] - EDGE, 0), min(keep[1] + EDGE, cols))
        used = [n for n, (low, high) in enumerate(parts) if low < window[1] and high > window[0]]
        mixed = conv_chunk(
            video, flags, [halos[2 * n + s] for n in used for s in (0, 1)],
            [parts[n] for n in used], window, keep, owners, conv_weights,
        )
        block = lax.all_to_all(mixed, "tm", split_axis=0, concat_axis=0, tiled=True)
        own = step // owners
        final = attend_chunk(
            block.reshape(owners * frames, rows * own, chans), attend_weights, 64, 16
        )
        final = final.reshape(owners, frames, rows, own, chans)
        back = lax.all_to_all(final, "tm", split_axis=0, concat_axis=0, tiled=True)
        outs.append(jnp.transpose(back, (1, 2, 0, 3, 4)).reshape(frames, rows, step, chans))
    return jnp.concatenate(outs, axis=2)


def solution(mesh):
    placed = (P("tm", "strip", None, None), P(), P(), P(), P(), P(), P(), P(), P(), P(), P(), P())
    return jax.shard_map(
        shards, mesh=mesh, in_specs=placed, out_specs=P("tm", "strip", None, None), check_vma=False
    )
```

time: 202 us -> 118 us (0.58)
  the two profiles are of different devices: /device:TPU:160 before, /device:TPU:66 now
where the time goes in v1:
time: 118 us
  waiting for transfers between devices  43.8 us (37%)
  starting transfers between devices  31.8 us (27%)
  Pallas kernels  29.9 us (25%)
  local copies, waits for them, and re-layouts  10.4 us (9%)
  other arithmetic  1.54 us (1%)
    all_to_all x2, waiting for transfers between devices, shards(): back = lax.all_to_all(final, 'tm', split_axis=0, concat_axis=0, tiled=True)  22.9 us
    pallas_call x2, Pallas kernels, conv_chunk(): pl.pallas_call(functools.partial(conv_body, plan), grid=(frames,), in_spe...  17.1 us
    pallas_call x2, Pallas kernels, attend_chunk(): pl.pallas_call(functools.partial(attend_body, group), grid=(pixels // til...  12.8 us
    all_to_all x2, starting transfers between devices, shards(): block = lax.all_to_all(mixed, 'tm', split_axis=0, concat_axis=0, tiled=True)  12.6 us
    ppermute x2, waiting for transfers between devices, shards(): halos.append(lax.ppermute(video[:, :2, low:high], 'strip', backward))  9.27 us
    all_to_all x2, starting transfers between devices, shards(): back = lax.all_to_all(final, 'tm', split_axis=0, concat_axis=0, tiled=True)  9.05 us
    all_to_all x2, waiting for transfers between devices, shards(): block = lax.all_to_all(mixed, 'tm', split_axis=0, concat_axis=0, tiled=True)  8.88 us
    unnamed x34, local copies, waits for them, and re-layouts  5.8 us
  transfers between devices with their start and end apart: 8, of which 6 were waited for; matrix products, arithmetic and copies ran while one was open for 2% of the time, Pallas kernels for 25%

profile of v1, /device:TPU:66, one launch (start us, length us, event | category | flops | bytes accessed | tf_op | source)
XLA Modules:
  0.0 117.7 jit_solution(17050548144165583462)
XLA Ops:
  0.0 2.5 %fusion.1 = (bf16[2,2,272,256]{3,2,1,0:T(8,128)(2,1)}, bf16[2,2,272,256]{3,2,1,0:T(8,128)(2,1)}) fusion(bf16[2,4,512,256]{3,2,1,0:T(8,128)(2,1)} %video.3), kind=kLoop, calls=%fused_computation.3 | loop fusion | bytes 2228224 | tf_op jit(solution)/shard_map/slice | solution.py:214
  2.5 1.9 %collective-permute-start.1 = (bf16[2,2,272,256]{3,2,1,0:T(8,128)(2,1)}, bf16[2,2,272,256]{3,2,1,0:T(8,128)(2,1)}, u32[]{:S(2)}, u32[]{:S(2)}) collective-permute-start(bf16[2,2,272,256]{3,2,1,0:T(8,128)(2,1)} %get-tuple-element.7), channel_id=1, source_target_pairs={{1,0},{2,1},{3,2},{4,3},{5,4},{6,5},{7,6},{8,7},{9,8},{10,9},{11,1... | collective-permute-start | bytes 1671176 | tf_op jit(solution)/shard_map/ppermute | solution.py:214
  4.4 2.4 %collective-permute-start = (bf16[2,2,272,256]{3,2,1,0:T(8,128)(2,1)}, bf16[2,2,272,256]{3,2,1,0:T(8,128)(2,1)}, u32[]{:S(2)}, u32[]{:S(2)}) collective-permute-start(bf16[2,2,272,256]{3,2,1,0:T(8,128)(2,1)} %get-tuple-element.8), channel_id=1, source_target_pairs={{0,1},{1,2},{2,3},{3,4},{4,5},{5,6},{6,7},{7,8},{8,9},{9,10},{10,1... | collective-permute-start | bytes 1671176 | tf_op jit(solution)/shard_map/ppermute | solution.py:213
  6.8 1.0 fusion
  7.8 3.1 %collective-permute-start.3 = (bf16[2,2,240,256]{3,2,1,0:T(8,128)(2,1)}, bf16[2,2,240,256]{3,2,1,0:T(8,128)(2,1)}, u32[]{:S(2)}, u32[]{:S(2)}) collective-permute-start(bf16[2,2,240,256]{3,2,1,0:T(8,128)(2,1)} %get-tuple-element.5), channel_id=1, source_target_pairs={{1,0},{2,1},{3,2},{4,3},{5,4},{6,5},{7,6},{8,7},{9,8},{10,9},{11,1... | collective-permute-start | bytes 1474568 | tf_op jit(solution)/shard_map/ppermute | solution.py:214
  11.0 2.6 %collective-permute-start.2 = (bf16[2,2,240,256]{3,2,1,0:T(8,128)(2,1)}, bf16[2,2,240,256]{3,2,1,0:T(8,128)(2,1)}, u32[]{:S(2)}, u32[]{:S(2)}) collective-permute-start(bf16[2,2,240,256]{3,2,1,0:T(8,128)(2,1)} %get-tuple-element.6), channel_id=1, source_target_pairs={{0,1},{1,2},{2,3},{3,4},{4,5},{5,6},{6,7},{7,8},{8,9},{9,10},{10,1... | collective-permute-start | bytes 1474568 | tf_op jit(solution)/shard_map/ppermute | solution.py:213
  13.6 0.1 add_convert_fusion.flags
  13.7 9.3 %collective-permute-done.1.refs_1_ = bf16[2,2,272,256]{3,2,1,0:T(8,128)(2,1)} collective-permute-done((bf16[2,2,272,256]{3,2,1,0:T(8,128)(2,1)}, bf16[2,2,272,256]{3,2,1,0:T(8,128)(2,1)}, u32[]{:S(2)}, u32[]{:S(2)}) %collective-permute-start.1) | collective-permute-done | bytes 557088 | tf_op jit(solution)/shard_map/ppermute | solution.py:214
  23.0 2.8 %collective-permute-done.refs_0_ = bf16[2,2,272,256]{3,2,1,0:T(8,128)(2,1)} collective-permute-done((bf16[2,2,272,256]{3,2,1,0:T(8,128)(2,1)}, bf16[2,2,272,256]{3,2,1,0:T(8,128)(2,1)}, u32[]{:S(2)}, u32[]{:S(2)}) %collective-permute-start) | collective-permute-done | bytes 557088 | tf_op jit(solution)/shard_map/ppermute | solution.py:213
  25.8 0.0 copy-start.5
  25.8 1.3 %copy-done.5 = bf16[3,3,256,256]{3,2,1,0:T(8,128)(2,1)S(1)} copy-done((bf16[3,3,256,256]{3,2,1,0:T(8,128)(2,1)S(1)}, bf16[3,3,256,256]{3,2,1,0:T(8,128)(2,1)}, u32[]{:S(2)}) %copy-start.5) | copy-done | bytes 1179672
  27.1 8.5 %convs.2 = bf16[8,2,4,32,256]{4,3,2,1,0:T(8,128)(2,1)S(1)} custom-call(f32[2]{0:T(128)S(1)} %add_convert_fusion.flags, bf16[2,4,512,256]{3,2,1,0:T(8,128)(2,1)S(1)} %copy-done, bf16[2,2,272,256]{3,2,1,0:T(8,128)(2,1)} %collective-permute-done.refs_0_, bf16[2,2,272,256]{3,2,1,0:T(8,128)(2,1)} %collective-permute-done.1.refs_1_, f32[1,256]{1,0:T(1,128)S(1)} %bitcast.25, ...), custom_call_target="tpu_custom_call" | custom-call | flops 6417285120 | bytes 8388608 | tf_op jit(solution)/shard_map/convs/pallas_call | solution.py:93
  35.6 1.0 copy-done.1
  36.5 6.0 %all-to-all-start = ((bf16[8,2,4,32,256]{4,3,2,1,0:T(8,128)(2,1)}), bf16[8,2,4,32,256]{4,3,2,1,0:T(8,128)(2,1)S(1)}, u32[]{:S(2)}, u32[]{:S(2)}) async-start(bf16[8,2,4,32,256]{4,3,2,1,0:T(8,128)(2,1)} %copy-done.1), calls=%async_computation | async-start | bytes 2097152 | tf_op jit(solution)/shard_map/all_to_all | solution.py:225
  42.6 1.3 %copy-done.4 = bf16[3,3,256,256]{3,2,1,0:T(8,128)(2,1)S(1)} copy-done((bf16[3,3,256,256]{3,2,1,0:T(8,128)(2,1)S(1)}, bf16[3,3,256,256]{3,2,1,0:T(8,128)(2,1)}, u32[]{:S(2)}) %copy-start.4) | copy-done | bytes 1179672
  43.9 1.3 %copy-done.6 = bf16[3,3,256,256]{3,2,1,0:T(8,128)(2,1)S(1)} copy-done((bf16[3,3,256,256]{3,2,1,0:T(8,128)(2,1)S(1)}, bf16[3,3,256,256]{3,2,1,0:T(8,128)(2,1)}, u32[]{:S(2)}) %copy-start.6) | copy-done | bytes 1179672
  45.1 8.6 %convs.3 = bf16[8,2,4,32,256]{4,3,2,1,0:T(8,128)(2,1)S(1)} custom-call(f32[2]{0:T(128)S(1)} %add_convert_fusion.flags, bf16[2,4,512,256]{3,2,1,0:T(8,128)(2,1)S(1)} %copy-done, bf16[2,2,272,256]{3,2,1,0:T(8,128)(2,1)} %collective-permute-done.refs_0_, bf16[2,2,272,256]{3,2,1,0:T(8,128)(2,1)} %collective-permute-done.1.refs_1_, ...), custom_call_target="tpu_custom_call" | custom-call | flops 6417285120 | bytes 8388608 | tf_op jit(solution)/shard_map/convs/pallas_call | solution.py:93
  53.8 0.0 copy-start.2
  53.8 1.0 copy-done.2
  54.8 0.0 copy-start.15
  54.8 0.8 all-to-all-done
  55.6 6.6 %all-to-all-start.2 = ((bf16[8,2,4,32,256]{4,3,2,1,0:T(8,128)(2,1)}), bf16[8,2,4,32,256]{4,3,2,1,0:T(8,128)(2,1)S(1)}, u32[]{:S(2)}, u32[]{:S(2)}) async-start(bf16[8,2,4,32,256]{4,3,2,1,0:T(8,128)(2,1)} %copy-done.2), calls=%async_computation.2 | async-start | bytes 2097152 | tf_op jit(solution)/shard_map/all_to_all | solution.py:225
  62.2 6.4 %attend.2 = bf16[16,128,256]{2,1,0:T(8,128)(2,1)} custom-call(bf16[16,128,256]{2,1,0:T(8,128)(2,1)S(1)} %bitcast.17, f32[1,256]{1,0:T(1,128)S(1)} %bitcast.29, bf16[768,256]{1,0:T(8,128)(2,1)S(1)} %bitcast.23, f32[1,256]{1,0:T(1,128)S(1)} %bitcast.31, bf16[256,256]{1,0:T(8,128)(2,1)S(1)} %copy-done.8, bf16[256,256]{1,0:T(8,128)(2,1)S(1)} %copy-done.9, ...), custom_call_target="tpu_custom_call" | custom-call | flops 2415919104 | bytes 4194304 | tf_op jit(solution)/shard_map/attend/pallas_call | solution.py:162
  68.6 8.1 %all-to-all-done.2 = bf16[8,2,4,32,256]{4,3,2,1,0:T(8,128)(2,1)S(1)} async-done(((bf16[8,2,4,32,256]{4,3,2,1,0:T(8,128)(2,1)}), bf16[8,2,4,32,256]{4,3,2,1,0:T(8,128)(2,1)S(1)}, u32[]{:S(2)}, u32[]{:S(2)}) %all-to-all-start.2) | async-done | bytes 1048608 | tf_op jit(solution)/shard_map/all_to_all | solution.py:225
  76.8 5.1 %all-to-all-start.1 = ((bf16[8,2,4,32,256]{4,3,2,1,0:T(8,128)(2,1)}), bf16[8,2,4,32,256]{4,3,2,1,0:T(8,128)(2,1)S(1)}, u32[]{:S(2)}, u32[]{:S(2)}) async-start(bf16[8,2,4,32,256]{4,3,2,1,0:T(8,128)(2,1)} %bitcast.10), calls=%async_computation.1 | async-start | bytes 2097152 | tf_op jit(solution)/shard_map/all_to_all | solution.py:231
  81.9 6.4 %attend.3 = bf16[16,128,256]{2,1,0:T(8,128)(2,1)} custom-call(bf16[16,128,256]{2,1,0:T(8,128)(2,1)S(1)} %bitcast.18, f32[1,256]{1,0:T(1,128)S(1)} %bitcast.30, bf16[768,256]{1,0:T(8,128)(2,1)S(1)} %bitcast.24, f32[1,256]{1,0:T(1,128)S(1)} %bitcast.32, bf16[256,256]{1,0:T(8,128)(2,1)S(1)} %copy-done.8, bf16[256,256]{1,0:T(8,128)(2,1)S(1)} %copy-done.9, ...), custom_call_target="tpu_custom_call" | custom-call | flops 2415919104 | bytes 4194304 | tf_op jit(solution)/shard_map/attend/pallas_call | solution.py:162
  88.3 10.9 %all-to-all-done.1 = bf16[8,2,4,32,256]{4,3,2,1,0:T(8,128)(2,1)S(1)} async-done(((bf16[8,2,4,32,256]{4,3,2,1,0:T(8,128)(2,1)}), bf16[8,2,4,32,256]{4,3,2,1,0:T(8,128)(2,1)S(1)}, u32[]{:S(2)}, u32[]{:S(2)}) %all-to-all-start.1) | async-done | bytes 1048608 | tf_op jit(solution)/shard_map/all_to_all | solution.py:231
  99.2 3.9 %all-to-all-start.3 = ((bf16[8,2,4,32,256]{4,3,2,1,0:T(8,128)(2,1)}), bf16[8,2,4,32,256]{4,3,2,1,0:T(8,128)(2,1)S(1)}, u32[]{:S(2)}, u32[]{:S(2)}) async-start(bf16[8,2,4,32,256]{4,3,2,1,0:T(8,128)(2,1)} %bitcast.14), calls=%async_computation.3 | async-start | bytes 2097152 | tf_op jit(solution)/shard_map/all_to_all | solution.py:231
  103.1 1.1 copy.13
  104.2 11.9 %all-to-all-done.3 = bf16[8,2,4,32,256]{4,3,2,1,0:T(8,128)(2,1)S(1)} async-done(((bf16[8,2,4,32,256]{4,3,2,1,0:T(8,128)(2,1)}), bf16[8,2,4,32,256]{4,3,2,1,0:T(8,128)(2,1)S(1)}, u32[]{:S(2)}, u32[]{:S(2)}) %all-to-all-start.3) | async-done | bytes 1048608 | tf_op jit(solution)/shard_map/all_to_all | solution.py:231
  116.1 0.1 copy.14
  116.2 1.5 %pad_maximum_fusion = bf16[2,4,512,256]{3,2,1,0:T(8,128)(2,1)} fusion(bf16[2,4,256,256]{3,2,1,0:T(8,128)(2,1)S(1)} %bitcast.36, bf16[2,4,256,256]{3,2,1,0:T(8,128)(2,1)S(1)} %bitcast.35), kind=kLoop, calls=%fused_computation | loop fusion | flops 4194304 | bytes 4194304 | tf_op jit(solution)/shard_map/concatenate | solution.py:233
  (28 shorter events, 0.1 us)
Async XLA Ops:
  0.0 6.8 %copy-start = (bf16[2,4,512,256]{3,2,1,0:T(8,128)(2,1)S(1)}, bf16[2,4,512,256]{3,2,1,0:T(8,128)(2,1)}, u32[]{:S(2)}) copy-start(bf16[2,4,512,256]{3,2,1,0:T(8,128)(2,1)} %video.3) | copy-start | bytes 6291460
  0.0 25.8 %copy-start.13 = (f32[256]{0:T(256)S(1)}, f32[256]{0:T(256)}, u32[]{:S(2)}) copy-start(f32[256]{0:T(256)} %param.15) | copy-start | bytes 3076
  0.0 25.8 %copy-start.3 = (bf16[3,3,256,256]{3,2,1,0:T(8,128)(2,1)S(1)}, bf16[3,3,256,256]{3,2,1,0:T(8,128)(2,1)}, u32[]{:S(2)}) copy-start(bf16[3,3,256,256]{3,2,1,0:T(8,128)(2,1)} %param.14) | copy-start | bytes 3538948
  0.0 25.8 %copy-start.12 = (f32[256]{0:T(256)S(1)}, f32[256]{0:T(256)}, u32[]{:S(2)}) copy-start(f32[256]{0:T(256)} %param.13) | copy-start | bytes 3076
  2.5 20.5 %collective-permute-start.1 = (bf16[2,2,272,256]{3,2,1,0:T(8,128)(2,1)}, bf16[2,2,272,256]{3,2,1,0:T(8,128)(2,1)}, u32[]{:S(2)}, u32[]{:S(2)}) collective-permute-start(bf16[2,2,272,256]{3,2,1,0:T(8,128)(2,1)} %get-tuple-element.7), channel_id=1, source_target_pairs={{1,0},{2,1},{3,2},{4,3},{5,4},{6,5},{7,6},{8,7},{9,8},{10,9},{11,1... | collective-permute-start | bytes 1671176 | tf_op jit(solution)/shard_map/ppermute | solution.py:214
  4.4 21.4 %collective-permute-start = (bf16[2,2,272,256]{3,2,1,0:T(8,128)(2,1)}, bf16[2,2,272,256]{3,2,1,0:T(8,128)(2,1)}, u32[]{:S(2)}, u32[]{:S(2)}) collective-permute-start(bf16[2,2,272,256]{3,2,1,0:T(8,128)(2,1)} %get-tuple-element.8), channel_id=1, source_target_pairs={{0,1},{1,2},{2,3},{3,4},{4,5},{5,6},{6,7},{7,8},{8,9},{9,10},{10,1... | collective-permute-start | bytes 1671176 | tf_op jit(solution)/shard_map/ppermute | solution.py:213
  7.8 34.8 %collective-permute-start.3 = (bf16[2,2,240,256]{3,2,1,0:T(8,128)(2,1)}, bf16[2,2,240,256]{3,2,1,0:T(8,128)(2,1)}, u32[]{:S(2)}, u32[]{:S(2)}) collective-permute-start(bf16[2,2,240,256]{3,2,1,0:T(8,128)(2,1)} %get-tuple-element.5), channel_id=1, source_target_pairs={{1,0},{2,1},{3,2},{4,3},{5,4},{6,5},{7,6},{8,7},{9,8},{10,9},{11,1... | collective-permute-start | bytes 1474568 | tf_op jit(solution)/shard_map/ppermute | solution.py:214
  11.0 31.6 %collective-permute-start.2 = (bf16[2,2,240,256]{3,2,1,0:T(8,128)(2,1)}, bf16[2,2,240,256]{3,2,1,0:T(8,128)(2,1)}, u32[]{:S(2)}, u32[]{:S(2)}) collective-permute-start(bf16[2,2,240,256]{3,2,1,0:T(8,128)(2,1)} %get-tuple-element.6), channel_id=1, source_target_pairs={{0,1},{1,2},{2,3},{3,4},{4,5},{5,6},{6,7},{7,8},{8,9},{9,10},{10,1... | collective-permute-start | bytes 1474568 | tf_op jit(solution)/shard_map/ppermute | solution.py:213
  25.8 1.3 %copy-start.5 = (bf16[3,3,256,256]{3,2,1,0:T(8,128)(2,1)S(1)}, bf16[3,3,256,256]{3,2,1,0:T(8,128)(2,1)}, u32[]{:S(2)}) copy-start(bf16[3,3,256,256]{3,2,1,0:T(8,128)(2,1)} %param.16) | copy-start | bytes 3538948
  35.6 1.0 copy-start.1
  36.5 19.0 %all-to-all-start = ((bf16[8,2,4,32,256]{4,3,2,1,0:T(8,128)(2,1)}), bf16[8,2,4,32,256]{4,3,2,1,0:T(8,128)(2,1)S(1)}, u32[]{:S(2)}, u32[]{:S(2)}) async-start(bf16[8,2,4,32,256]{4,3,2,1,0:T(8,128)(2,1)} %copy-done.1), calls=%async_computation | async-start | bytes 2097152 | tf_op jit(solution)/shard_map/all_to_all | solution.py:225
  42.6 1.3 %copy-start.4 = (bf16[3,3,256,256]{3,2,1,0:T(8,128)(2,1)S(1)}, bf16[3,3,256,256]{3,2,1,0:T(8,128)(2,1)}, u32[]{:S(2)}) copy-start(bf16[3,3,256,256]{3,2,1,0:T(8,128)(2,1)} %param.14) | copy-start | bytes 3538948
  43.9 1.3 %copy-start.6 = (bf16[3,3,256,256]{3,2,1,0:T(8,128)(2,1)S(1)}, bf16[3,3,256,256]{3,2,1,0:T(8,128)(2,1)}, u32[]{:S(2)}) copy-start(bf16[3,3,256,256]{3,2,1,0:T(8,128)(2,1)} %param.16) | copy-start | bytes 3538948
  53.8 1.0 copy-start.2
  54.8 7.4 %copy-start.7 = (bf16[3,256,256]{2,1,0:T(8,128)(2,1)S(1)}, bf16[3,256,256]{2,1,0:T(8,128)(2,1)}, u32[]{:S(2)}) copy-start(bf16[3,256,256]{2,1,0:T(8,128)(2,1)} %param.18) | copy-start | bytes 1179652
  54.8 7.4 %copy-start.8 = (bf16[256,256]{1,0:T(8,128)(2,1)S(1)}, bf16[256,256]{1,0:T(8,128)(2,1)}, u32[]{:S(2)}) copy-start(bf16[256,256]{1,0:T(8,128)(2,1)} %wq.3) | copy-start | bytes 393220
  54.8 7.4 %copy-start.9 = (bf16[256,256]{1,0:T(8,128)(2,1)S(1)}, bf16[256,256]{1,0:T(8,128)(2,1)}, u32[]{:S(2)}) copy-start(bf16[256,256]{1,0:T(8,128)(2,1)} %wk.3) | copy-start | bytes 393220
  54.8 7.4 %copy-start.10 = (bf16[256,256]{1,0:T(8,128)(2,1)S(1)}, bf16[256,256]{1,0:T(8,128)(2,1)}, u32[]{:S(2)}) copy-start(bf16[256,256]{1,0:T(8,128)(2,1)} %wv.3) | copy-start | bytes 393220
  54.8 7.4 %copy-start.11 = (bf16[256,256]{1,0:T(8,128)(2,1)S(1)}, bf16[256,256]{1,0:T(8,128)(2,1)}, u32[]{:S(2)}) copy-start(bf16[256,256]{1,0:T(8,128)(2,1)} %wo.3) | copy-start | bytes 393220
  54.8 7.4 %copy-start.14 = (f32[256]{0:T(256)S(1)}, f32[256]{0:T(256)}, u32[]{:S(2)}) copy-start(f32[256]{0:T(256)} %param.17) | copy-start | bytes 3076
  54.8 7.4 %copy-start.15 = (f32[256]{0:T(256)S(1)}, f32[256]{0:T(256)}, u32[]{:S(2)}) copy-start(f32[256]{0:T(256)} %param.19) | copy-start | bytes 3076
  55.6 21.2 %all-to-all-start.2 = ((bf16[8,2,4,32,256]{4,3,2,1,0:T(8,128)(2,1)}), bf16[8,2,4,32,256]{4,3,2,1,0:T(8,128)(2,1)S(1)}, u32[]{:S(2)}, u32[]{:S(2)}) async-start(bf16[8,2,4,32,256]{4,3,2,1,0:T(8,128)(2,1)} %copy-done.2), calls=%async_computation.2 | async-start | bytes 2097152 | tf_op jit(solution)/shard_map/all_to_all | solution.py:225
  76.8 22.5 %all-to-all-start.1 = ((bf16[8,2,4,32,256]{4,3,2,1,0:T(8,128)(2,1)}), bf16[8,2,4,32,256]{4,3,2,1,0:T(8,128)(2,1)S(1)}, u32[]{:S(2)}, u32[]{:S(2)}) async-start(bf16[8,2,4,32,256]{4,3,2,1,0:T(8,128)(2,1)} %bitcast.10), calls=%async_computation.1 | async-start | bytes 2097152 | tf_op jit(solution)/shard_map/all_to_all | solution.py:231
  99.2 16.9 %all-to-all-start.3 = ((bf16[8,2,4,32,256]{4,3,2,1,0:T(8,128)(2,1)}), bf16[8,2,4,32,256]{4,3,2,1,0:T(8,128)(2,1)S(1)}, u32[]{:S(2)}, u32[]{:S(2)}) async-start(bf16[8,2,4,32,256]{4,3,2,1,0:T(8,128)(2,1)} %bitcast.14), calls=%async_computation.3 | async-start | bytes 2097152 | tf_op jit(solution)/shard_map/all_to_all | solution.py:231
  104.2 12.0 %copy-start.16 = (bf16[2,4,8,32,256]{4,3,2,1,0:T(8,128)(2,1)S(1)}, bf16[2,4,8,32,256]{4,3,2,1,0:T(8,128)(2,1)}, u32[]{:S(2)}) copy-start(bf16[2,4,8,32,256]{4,3,2,1,0:T(8,128)(2,1)} %copy.13) | copy-start | bytes 3145732

commit v2 on v1

v2 whole, which is shorter than its diff:
```python
import functools

import jax
import jax.numpy as jnp
from jax import lax
from jax.experimental import pallas as pl
from jax.experimental.pallas import tpu as pltpu
from jax.sharding import PartitionSpec as P

BF16 = jnp.bfloat16
F32 = jnp.float32
EPS = 1e-06
HALF = 2


def scaled(values, gain):
    mean = jnp.mean(values * values, axis=-1, keepdims=True)
    return values * lax.rsqrt(mean + EPS) * gain


def silu_from_half(half):
    return half + half * jnp.tanh(half)


def put_shifted(dst, row, values):
    width, chans = values.shape
    index = lax.broadcasted_iota(jnp.int32, (width, 1), 0)
    before = jnp.where(index == 0, 0.0, pltpu.roll(values, 1, 0))
    after = jnp.where(index == width - 1, 0.0, pltpu.roll(values, width - 1, 0))
    dst[row, :, 0:chans] = before.astype(BF16)
    dst[row, :, chans : 2 * chans] = values.astype(BF16)
    dst[row, :, 2 * chans : 3 * chans] = after.astype(BF16)


def product(source, weights, row):
    lhs = jnp.concatenate([source[row + i] for i in range(3)], axis=-1)
    return jnp.dot(lhs, weights[...], preferred_element_type=F32)


def send(base, change, frame, index, held, out, sems):
    mixed = (base.astype(F32) + change).astype(BF16)
    held[frame, index] = mixed.reshape(held.shape[2:])
    copy = pltpu.make_async_copy(
        held.at[frame, index], out.at[:, frame, index], sems.at[frame, index]
    )
    copy.start()
    return copy


def inner_body(info, inner, outer, halo, gain_one, w_one, gain_two, conv_two,
               out, shared, s_one, s_two, w_two, kept, held, w_sem, kept_sems, sems):
    frames, _, width, chans = inner.shape
    odd = info[0] == 1
    half_one = gain_one[...] * 0.5
    half_two = gain_two[...] * 0.5
    load = pltpu.make_async_copy(conv_two, w_two, w_sem)
    load.start()

    def put_first(frame, index):
        if index < HALF:
            raw = jnp.where(odd, halo[frame, index], outer[frame, index])
        elif index < 2 * HALF:
            raw = inner[frame, index - HALF]
        else:
            raw = jnp.where(odd, outer[frame, index - 2 * HALF], halo[frame, index - 2 * HALF])
        put_shifted(s_one.at[frame], index, silu_from_half(scaled(raw.astype(F32), half_one)))

    def put_second(frame, index):
        hidden = product(s_one.at[frame], w_one, index)
        put_shifted(s_two.at[frame], index, silu_from_half(scaled(hidden, half_two)))

    for index in range(3 * HALF):
        put_first(0, index)
    copies = []
    for frame in range(frames):
        for index in range(2 * HALF):
            if frame + 1 < frames:
                for ahead in range(index * 3 // 2, (index + 1) * 3 // 2):
                    put_first(frame + 1, ahead)
            put_second(frame, index)
    load.wait()
    for frame in range(frames):
        here = slice(chans, 2 * chans)
        for index in range(HALF):
            kept[frame, index] = jnp.where(
                odd, s_two[frame, HALF + index, :, here], s_two[frame, index, :, here]
            )
        copy = pltpu.make_async_copy(kept.at[frame], shared.at[frame], kept_sems.at[frame])
        copy.start()
        copies.append(copy)
        for index in range(HALF):
            change = product(s_two.at[frame], w_two, index)
            copies.append(send(inner[frame, index], change, frame, index, held, out, sems))
    for copy in copies:
        copy.wait()


def outer_body(info, outer, halo, shared, gain_one, w_one, gain_two, conv_two,
               out, s_one, s_two_a, s_two_b, w_two, kept, held, w_sem, kept_sems, sems):
    frames, _, width, chans = outer.shape
    odd, goes_on = info[0] == 1, info[1] == 1
    new_at = jnp.where(odd, HALF, 0)
    shared_at = HALF - new_at
    half_one = gain_one[...] * 0.5
    half_two = gain_two[...] * 0.5
    s_two = (s_two_a, s_two_b)
    fetch = pltpu.make_async_copy(shared, kept, kept_sems.at[0])
    load = pltpu.make_async_copy(conv_two, w_two, w_sem)
    fetch.start()
    load.start()

    def put_first(frame, index):
        if index < HALF:
            raw = jnp.where(odd, outer[frame, index], halo[frame, index])
        else:
            raw = jnp.where(odd, halo[frame, index - HALF], outer[frame, index - HALF])
        put_shifted(s_one.at[frame], index, silu_from_half(scaled(raw.astype(F32), half_one)))

    def put_second(frame, index):
        hidden = product(s_one.at[frame], w_one, index)
        second = silu_from_half(scaled(hidden, half_two))
        outside = jnp.logical_not(goes_on) & (odd if index == HALF - 1 else jnp.logical_not(odd))
        second = jnp.where(outside, 0.0, second)
        put_shifted(s_two[frame], new_at + index, second)

    for index in range(2 * HALF):
        put_first(0, index)
    for frame in range(frames):
        for index in range(HALF):
            if frame + 1 < frames:
                for ahead in range(2 * index, 2 * index + 2):
                    put_first(frame + 1, ahead)
            put_second(frame, index)
        if frame == 0:
            fetch.wait()
            load.wait()
        for index in range(HALF):
            put_shifted(s_two[frame], shared_at + index, kept[frame, index].astype(F32))
    copies = []
    for frame in range(frames):
        for index in range(HALF):
            change = product(s_two[frame], w_two, index)
            copies.append(send(outer[frame, index], change, frame, index, held, out, sems))
    for copy in copies:
        copy.wait()


def conv_chunk(info, inner, outer, halo, shared, owners, weights):
    frames, _, cols, chans = outer.shape
    own = cols // owners
    is_outer = shared is not None
    stack = lambda count: pltpu.VMEM((frames, count, cols, 3 * chans), BF16)
    here = pl.BlockSpec(memory_space=pltpu.VMEM)
    there = pl.BlockSpec(memory_space=pltpu.HBM)
    near = lambda v: pltpu.with_memory_space_constraint(v, pltpu.VMEM)
    far = lambda v: pltpu.with_memory_space_constraint(v, pltpu.HBM)
    gain_one, conv_one, gain_two, conv_two = weights
    mixed = pltpu.HBM((owners, frames, HALF, own, chans), BF16)
    keep = pltpu.HBM((frames, HALF, cols, chans), BF16)
    first_rows = (2 if is_outer else 3) * HALF
    new_rows = (1 if is_outer else 2) * HALF
    flops = 2 * frames * (new_rows + HALF) * cols * 9 * chans * chans
    two = [pltpu.VMEM((2 * HALF, cols, 3 * chans), BF16)] * 2 if is_outer else [stack(2 * HALF)]
    return pl.pallas_call(
        outer_body if is_outer else inner_body,
        in_specs=[
            pl.BlockSpec(memory_space=pltpu.SMEM), here, here, there if is_outer else here,
            here, here, here, there,
        ],
        out_specs=[there] if is_outer else [there, there],
        out_shape=[mixed] if is_outer else [mixed, keep],
        scratch_shapes=[
            stack(first_rows),
            *two,
            pltpu.VMEM(conv_two.shape, BF16),
            pltpu.VMEM((frames, HALF, cols, chans), BF16),
            pltpu.VMEM((frames, HALF, owners, own, chans), BF16),
            pltpu.SemaphoreType.DMA,
            pltpu.SemaphoreType.DMA((frames,)),
            pltpu.SemaphoreType.DMA((frames, HALF)),
        ],
        compiler_params=pltpu.CompilerParams(vmem_limit_bytes=28 * 1024 * 1024),
        cost_estimate=pl.CostEstimate(
            flops=flops, bytes_accessed=8 * 1024 * 1024, transcendentals=0
        ),
        name="convs_outer" if is_outer else "convs_inner",
    )(
        info, *((outer, halo, far(shared)) if is_outer else (inner, outer, halo)),
        gain_one, near(conv_one), gain_two, far(conv_two),
    )


def attend_body(group, x_ref, gain_three, kernel, gain_four, wq, wk, wv, wo, *refs):
    out_ref = refs[-1]
    frames, pixels, chans = x_ref.shape
    count = frames * pixels
    half_three = gain_three[...] * 0.5
    x = x_ref[...].reshape(count, chans).astype(F32)
    third = silu_from_half(scaled(x, half_three)).astype(BF16).reshape(frames, pixels, chans)
    one = jnp.concatenate([third[:1], third[:-1]], axis=0)
    two = jnp.concatenate([third[:1], third[:1], third[:-2]], axis=0)
    taps = jnp.concatenate([two, one, third], axis=-1).reshape(count, 3 * chans)
    timed = x + jnp.dot(taps, kernel[...], preferred_element_type=F32)
    fourth = scaled(timed, gain_four[...]).astype(BF16)
    project = lambda w: jnp.dot(fourth, w[...], preferred_element_type=F32)
    scale = 1.0 / float(chans) ** 0.5
    queries = (project(wq) * scale).astype(BF16).reshape(frames, pixels, chans)
    keys = project(wk).astype(BF16).reshape(frames, pixels, chans)
    values = project(wv).astype(BF16).reshape(frames, pixels, chans)
    size = frames * group
    down = lax.broadcasted_iota(jnp.int32, (size, size), 0)
    along = lax.broadcasted_iota(jnp.int32, (size, size), 1)
    allowed = (down % group == along % group) & (down >= along)
    pieces = []
    for g in range(pixels // group):
        cut = lambda v: v[:, g * group : (g + 1) * group].reshape(size, chans)
        scores = lax.dot_general(
            cut(queries), cut(keys), (((1,), (1,)), ((), ())), preferred_element_type=F32
        )
        scores = jnp.where(allowed, scores, -1e30)
        top = jnp.max(scores, axis=-1, keepdims=True)
        weights = jnp.exp(scores - top)
        total = jnp.sum(weights, axis=-1, keepdims=True)
        weights = (weights * (1.0 / total)).astype(BF16)
        attended = jnp.dot(weights, cut(values), preferred_element_type=F32)
        pieces.append(attended.astype(BF16).reshape(frames, group, chans))
    attended = pieces[0] if len(pieces) == 1 else jnp.concatenate(pieces, axis=1)
    final = timed + jnp.dot(
        attended.reshape(count, chans), wo[...], preferred_element_type=F32
    )
    out_ref[...] = final.astype(BF16).reshape(frames, pixels, chans)


def attend_chunk(x, weights, tile, group, result=None):
    frames, pixels, chans = x.shape
    tile = min(tile, pixels)
    skip = 0 if result is None else pixels // tile
    given = [] if result is None else [result]
    far = lambda v: pltpu.with_memory_space_constraint(v, pltpu.HBM)
    whole = lambda a: pl.BlockSpec(a.shape, lambda p: (0,) * a.ndim)
    return pl.pallas_call(
        functools.partial(attend_body, group),
        grid=(pixels // tile,),
        in_specs=[pl.BlockSpec((frames, tile, chans), lambda p: (0, p, 0))]
        + [whole(w) for w in weights]
        + [pl.BlockSpec(memory_space=pltpu.HBM)] * len(given),
        out_specs=pl.BlockSpec((frames, tile, chans), lambda p: (0, p + skip, 0)),
        out_shape=pltpu.HBM((frames, 2 * pixels, chans), BF16),
        input_output_aliases={1 + len(weights): 0} if given else {},
        compiler_params=pltpu.CompilerParams(vmem_limit_bytes=32 * 1024 * 1024),
        cost_estimate=pl.CostEstimate(
            flops=2 * frames * pixels * chans * chans * 9,
            bytes_accessed=4 * 1024 * 1024,
            transcendentals=0,
        ),
        name="attend",
    )(x, *[w if w.shape[0] == 1 else far(w) for w in weights], *given)


def place_body(starts, back, out, sems):
    owners, _, parts, rows, own, _ = back.shape
    copies = [
        pltpu.make_async_copy(
            back.at[o, :, n],
            out.at[:, pl.ds(starts[n], rows), pl.ds(o * own, own)],
            sems.at[n, o],
        )
        for o in range(owners)
        for n in range(parts)
    ]
    for copy in copies:
        copy.start()
    for copy in copies:
        copy.wait()


def place(starts, back, shape):
    owners, _, parts = back.shape[:3]
    return pl.pallas_call(
        place_body,
        in_specs=[
            pl.BlockSpec(memory_space=pltpu.SMEM), pl.BlockSpec(memory_space=pltpu.VMEM),
        ],
        out_specs=pl.BlockSpec(memory_space=pltpu.HBM),
        out_shape=pltpu.HBM(shape, BF16),
        scratch_shapes=[pltpu.SemaphoreType.DMA((parts, owners))],
        compiler_params=pltpu.CompilerParams(vmem_limit_bytes=16 * 1024 * 1024),
        cost_estimate=pl.CostEstimate(
            flops=0, bytes_accessed=4 * 1024 * 1024, transcendentals=0
        ),
        name="place",
    )(starts, back)


def split_body(starts, video, inner, outer, sems):
    copies = [
        pltpu.make_async_copy(video.at[:, pl.ds(starts[n], HALF)], part, sems.at[n])
        for n, part in ((1, outer), (0, inner))
    ]
    for copy in copies:
        copy.start()
    for copy in copies:
        copy.wait()


def split(starts, video):
    frames, rows, cols, chans = video.shape
    part = jax.ShapeDtypeStruct((frames, HALF, cols, chans), BF16)
    here = pl.BlockSpec(memory_space=pltpu.VMEM)
    return pl.pallas_call(
        split_body,
        in_specs=[
            pl.BlockSpec(memory_space=pltpu.SMEM), pl.BlockSpec(memory_space=pltpu.HBM),
        ],
        out_specs=[here, here],
        out_shape=[part, part],
        scratch_shapes=[pltpu.SemaphoreType.DMA((2,))],
        compiler_params=pltpu.CompilerParams(vmem_limit_bytes=8 * 1024 * 1024),
        cost_estimate=pl.CostEstimate(
            flops=0, bytes_accessed=4 * 1024 * 1024, transcendentals=0
        ),
        name="split",
    )(starts, pltpu.with_memory_space_constraint(video, pltpu.HBM))


def shards(
    video,
    gain_one,
    conv_one,
    gain_two,
    conv_two,
    gain_three,
    time_kernel,
    gain_four,
    query_weight,
    key_weight,
    value_weight,
    out_weight,
):
    owners = lax.axis_size("tm")
    strips = lax.axis_size("strip")
    strip = lax.axis_index("strip")
    chans = video.shape[-1]
    odd = strip % 2
    siblings = [(i, i ^ 1) for i in range(strips)]
    neighbours = [(i, i + 1 if i % 2 else i - 1) for i in range(1, strips - 1)]
    inner_start = HALF - HALF * odd
    outer_start = HALF * odd
    goes_on = (strip > 0) & (strip < strips - 1)
    info = jnp.stack([odd, goes_on.astype(jnp.int32)])
    row = lambda gain: gain.reshape(1, chans)
    flat = lambda w: w.reshape(-1, chans)
    conv_weights = (row(gain_one), flat(conv_one), row(gain_two), flat(conv_two))
    attend_weights = (
        row(gain_three), flat(time_kernel), row(gain_four),
        query_weight, key_weight, value_weight, out_weight,
    )
    starts = jnp.stack([inner_start, outer_start])
    inner, outer = split(starts, video)
    from_outer = lax.ppermute(outer, "strip", neighbours)
    from_sibling = lax.ppermute(inner, "strip", siblings)

    final = shared = None
    for halo in (from_sibling, from_outer):
        mixed, *kept = conv_chunk(info, inner, outer, halo, shared, owners, conv_weights)
        shared = kept[0] if kept else None
        block = lax.all_to_all(mixed, "tm", split_axis=0, concat_axis=0, tiled=True)
        frames = block.shape[0] * block.shape[1]
        final = attend_chunk(block.reshape(frames, -1, chans), attend_weights, 64, 16, final)
    final = final.reshape(owners, block.shape[1], 2, *block.shape[2:])
    back = lax.all_to_all(final, "tm", split_axis=0, concat_axis=0, tiled=True)
    return place(starts, back, video.shape)


def solution(mesh):
    placed = (P("tm", "strip", None, None), P(), P(), P(), P(), P(), P(), P(), P(), P(), P(), P())
    return jax.shard_map(
        shards, mesh=mesh, in_specs=placed, out_specs=P("tm", "strip", None, None), check_vma=False
    )
```

time: 118 us -> 109 us (0.924)
  the two profiles are of different devices: /device:TPU:66 before, /device:TPU:160 now
where the time goes in v2:
time: 109 us
  Pallas kernels  41.9 us (38%)
  blocking collectives  32.5 us (30%)
  waiting for transfers between devices  19.7 us (18%)
  starting transfers between devices  14.2 us (13%)
    all_to_all x1, blocking collectives, shards(): back = lax.all_to_all(final, 'tm', split_axis=0, concat_axis=0, tiled=True)  32.5 us
    pallas_call x2, Pallas kernels, conv_chunk(): pl.pallas_call(outer_body if is_outer else inner_body, in_specs=[pl.Block...  22.7 us
    all_to_all x2, waiting for transfers between devices, shards(): block = lax.all_to_all(mixed, 'tm', split_axis=0, concat_axis=0, tiled=True)  19.7 us
    pallas_call x2, Pallas kernels, attend_chunk(): pl.pallas_call(functools.partial(attend_body, group), grid=(pixels // til...  15.1 us
    all_to_all x2, starting transfers between devices, shards(): block = lax.all_to_all(mixed, 'tm', split_axis=0, concat_axis=0, tiled=True)  10.2 us
    ppermute x1, starting transfers between devices, shards(): from_outer = lax.ppermute(outer, 'strip', neighbours)  3.93 us
  transfers between devices with their start and end apart: 4, of which 2 were waited for; matrix products, arithmetic and copies ran while one was open for 0% of the time, Pallas kernels for 28%

profile of v2, /device:TPU:160, one launch (start us, length us, event | category | flops | bytes accessed | tf_op | source)
XLA Modules:
  0.0 108.8 jit_solution(7168895435810673978)
XLA Ops:
  0.0 0.0 copy-start.2
  0.0 0.0 copy-start
  0.0 0.0 copy-start.1
  0.0 0.1 pad_add_fusion.starts
  0.1 2.1 %split.1 = (bf16[2,2,512,256]{3,2,1,0:T(8,128)(2,1)S(1)}, bf16[2,2,512,256]{3,2,1,0:T(8,128)(2,1)S(1)}) custom-call(s32[2]{0:T(128)S(1)} %pad_add_fusion.starts, bf16[2,4,512,256]{3,2,1,0:T(8,128)(2,1)} %video.1), custom_call_target="tpu_custom_call" | custom-call | bytes 4194304 | tf_op jit(solution)/shard_map/split/pallas_call | solution.py:310
  2.2 0.1 collective-permute-start.1
  2.3 3.9 %collective-permute-start = (bf16[2,2,512,256]{3,2,1,0:T(8,128)(2,1)S(1)}, bf16[2,2,512,256]{3,2,1,0:T(8,128)(2,1)}, u32[]{:S(2)}, u32[]{:S(2)}) collective-permute-start(bf16[2,2,512,256]{3,2,1,0:T(8,128)(2,1)S(1)} %get-tuple-element.9.outer), channel_id=1, source_target_pairs={{1,2},{2,1},{3,4},{4,3},{5,6},{6,5},{7,8},{8,7},{9,10},{10,9},{11,... | collective-permute-start | bytes 3145736 | tf_op jit(solution)/shard_map/ppermute | solution.py:360
  6.3 0.1 pad_add_fusion.1.info
  6.3 0.0 collective-permute-done.1.halo
  6.3 0.0 copy-done.2
  6.3 0.0 copy-done
  6.3 0.0 copy-done.1
  6.4 13.0 %convs_inner.1 = (bf16[8,2,2,64,256]{4,3,2,1,0:T(8,128)(2,1)}, bf16[2,2,512,256]{3,2,1,0:T(8,128)(2,1)}) custom-call(s32[2]{0:T(128)S(1)} %pad_add_fusion.1.info, bf16[2,2,512,256]{3,2,1,0:T(8,128)(2,1)S(1)} %get-tuple-element.10.inner, bf16[2,2,512,256]{3,2,1,0:T(8,128)(2,1)S(1)} %get-tuple-element.9.outer, ...), custom_call_target="tpu_custom_call" | custom-call | flops 7247757312 | bytes 8388608 | tf_op jit(solution)/shard_map/convs_inner/pallas_call | solution.py:164
  19.4 6.7 %all-to-all-start.1 = ((bf16[8,2,2,64,256]{4,3,2,1,0:T(8,128)(2,1)}), bf16[8,2,2,64,256]{4,3,2,1,0:T(8,128)(2,1)S(1)}, u32[]{:S(2)}, u32[]{:S(2)}) async-start(bf16[8,2,2,64,256]{4,3,2,1,0:T(8,128)(2,1)} %get-tuple-element.12), calls=%async_computation.1 | async-start | bytes 2097152 | tf_op jit(solution)/shard_map/all_to_all | solution.py:367
  26.0 0.0 collective-permute-done.halo
  26.0 9.7 %convs_outer.1 = bf16[8,2,2,64,256]{4,3,2,1,0:T(8,128)(2,1)} custom-call(s32[2]{0:T(128)S(1)} %pad_add_fusion.1.info, bf16[2,2,512,256]{3,2,1,0:T(8,128)(2,1)S(1)} %get-tuple-element.9.outer, bf16[2,2,512,256]{3,2,1,0:T(8,128)(2,1)} %collective-permute-done.halo, bf16[2,2,512,256]{3,2,1,0:T(8,128)(2,1)} %get-tuple-element.11.shared, f32[1,256]{1,0:T(1,128)S(1)} %bitcast.19, ...), custom_call_target="tpu_custom_call" | custom-call | flops 4831838208 | bytes 8388608 | tf_op jit(solution)/shard_map/convs_outer/pallas_call | solution.py:164
  35.7 0.0 copy-start.3
  35.8 0.0 copy-start.4
  35.8 8.9 %all-to-all-done.1 = bf16[8,2,2,64,256]{4,3,2,1,0:T(8,128)(2,1)S(1)} async-done(((bf16[8,2,2,64,256]{4,3,2,1,0:T(8,128)(2,1)}), bf16[8,2,2,64,256]{4,3,2,1,0:T(8,128)(2,1)S(1)}, u32[]{:S(2)}, u32[]{:S(2)}) %all-to-all-start.1) | async-done | bytes 1048608 | tf_op jit(solution)/shard_map/all_to_all | solution.py:367
  44.7 3.6 %all-to-all-start = ((bf16[8,2,2,64,256]{4,3,2,1,0:T(8,128)(2,1)}), bf16[8,2,2,64,256]{4,3,2,1,0:T(8,128)(2,1)S(1)}, u32[]{:S(2)}, u32[]{:S(2)}) async-start(bf16[8,2,2,64,256]{4,3,2,1,0:T(8,128)(2,1)} %convs_outer.1), calls=%async_computation | async-start | bytes 2097152 | tf_op jit(solution)/shard_map/all_to_all | solution.py:367
  48.3 0.0 copy-done.3
  48.3 0.0 copy-done.4
  48.3 7.6 %attend.2.refs_0_ = bf16[16,256,256]{2,1,0:T(8,128)(2,1)} custom-call(bf16[16,128,256]{2,1,0:T(8,128)(2,1)S(1)} %bitcast.14, f32[1,256]{1,0:T(1,128)S(1)} %bitcast.22, bf16[768,256]{1,0:T(8,128)(2,1)} %bitcast.29, f32[1,256]{1,0:T(1,128)S(1)} %bitcast.24, bf16[256,256]{1,0:T(8,128)(2,1)} %wq.3, bf16[256,256]{1,0:T(8,128)(2,1)} %wk.3, bf16[256,256]{1,0:T(8,128)(2,1)} %wv.3, ...), custom_call_target="tpu_custom_call" | custom-call | flops 2415919104 | bytes 4194304 | tf_op jit(solution)/shard_map/attend/pallas_call | solution.py:241
  55.9 10.7 %all-to-all-done = bf16[8,2,2,64,256]{4,3,2,1,0:T(8,128)(2,1)S(1)} async-done(((bf16[8,2,2,64,256]{4,3,2,1,0:T(8,128)(2,1)}), bf16[8,2,2,64,256]{4,3,2,1,0:T(8,128)(2,1)S(1)}, u32[]{:S(2)}, u32[]{:S(2)}) %all-to-all-start) | async-done | bytes 1048608 | tf_op jit(solution)/shard_map/all_to_all | solution.py:367
  66.6 7.5 %attend.3 = bf16[16,256,256]{2,1,0:T(8,128)(2,1)} custom-call(bf16[16,128,256]{2,1,0:T(8,128)(2,1)S(1)} %bitcast.15, f32[1,256]{1,0:T(1,128)S(1)} %bitcast.23, bf16[768,256]{1,0:T(8,128)(2,1)} %bitcast.30, f32[1,256]{1,0:T(1,128)S(1)} %bitcast.25, bf16[256,256]{1,0:T(8,128)(2,1)} %wq.3, bf16[256,256]{1,0:T(8,128)(2,1)} %wk.3, ...), custom_call_target="tpu_custom_call", output_to_operand_aliasing={{}: (8, {})} | custom-call | flops 2415919104 | bytes 4194304 | tf_op jit(solution)/shard_map/attend/pallas_call | solution.py:241
  74.1 32.5 %all_to_all.15.back = bf16[8,2,2,2,64,256]{5,4,3,2,1,0:T(8,128)(2,1)S(1)} all-to-all(bf16[8,2,2,2,64,256]{5,4,3,2,1,0:T(8,128)(2,1)} %bitcast.26), channel_id=1, replica_groups=mesh['tm'=8,'strip'=32] {'tm'}, dimensions={0} | all-to-all | bytes 4194304 | tf_op jit(solution)/shard_map/all_to_all | solution.py:371
  106.6 2.0 %place.1 = bf16[2,4,512,256]{3,2,1,0:T(8,128)(2,1)} custom-call(s32[2]{0:T(128)S(1)} %pad_add_fusion.starts, bf16[8,2,2,2,64,256]{5,4,3,2,1,0:T(8,128)(2,1)S(1)} %all_to_all.15.back), custom_call_target="tpu_custom_call" | custom-call | bytes 4194304 | tf_op jit(solution)/shard_map/place/pallas_call | solution.py:279
Async XLA Ops:
  0.0 6.3 %copy-start.2 = (f32[256]{0:T(256)S(1)}, f32[256]{0:T(256)}, u32[]{:S(2)}) copy-start(f32[256]{0:T(256)} %param.15) | copy-start | bytes 3076
  0.0 6.3 %copy-start = (bf16[3,3,256,256]{3,2,1,0:T(8,128)(2,1)S(1)}, bf16[3,3,256,256]{3,2,1,0:T(8,128)(2,1)}, u32[]{:S(2)}) copy-start(bf16[3,3,256,256]{3,2,1,0:T(8,128)(2,1)} %param.14) | copy-start | bytes 3538948
  0.0 6.3 %copy-start.1 = (f32[256]{0:T(256)S(1)}, f32[256]{0:T(256)}, u32[]{:S(2)}) copy-start(f32[256]{0:T(256)} %param.13) | copy-start | bytes 3076
  2.2 4.1 %collective-permute-start.1 = (bf16[2,2,512,256]{3,2,1,0:T(8,128)(2,1)S(1)}, bf16[2,2,512,256]{3,2,1,0:T(8,128)(2,1)}, u32[]{:S(2)}, u32[]{:S(2)}) collective-permute-start(bf16[2,2,512,256]{3,2,1,0:T(8,128)(2,1)S(1)} %get-tuple-element.10.inner), channel_id=1, source_target_pairs={{0,1},{1,0},{2,3},{3,2},{4,5},{5,4},{6,7},{7,6},{8,9},{9,8},{10,11... | collective-permute-start | bytes 3145736 | tf_op jit(solution)/shard_map/ppermute | solution.py:361
  2.3 23.7 %collective-permute-start = (bf16[2,2,512,256]{3,2,1,0:T(8,128)(2,1)S(1)}, bf16[2,2,512,256]{3,2,1,0:T(8,128)(2,1)}, u32[]{:S(2)}, u32[]{:S(2)}) collective-permute-start(bf16[2,2,512,256]{3,2,1,0:T(8,128)(2,1)S(1)} %get-tuple-element.9.outer), channel_id=1, source_target_pairs={{1,2},{2,1},{3,4},{4,3},{5,6},{6,5},{7,8},{8,7},{9,10},{10,9},{11,... | collective-permute-start | bytes 3145736 | tf_op jit(solution)/shard_map/ppermute | solution.py:360
  19.4 25.3 %all-to-all-start.1 = ((bf16[8,2,2,64,256]{4,3,2,1,0:T(8,128)(2,1)}), bf16[8,2,2,64,256]{4,3,2,1,0:T(8,128)(2,1)S(1)}, u32[]{:S(2)}, u32[]{:S(2)}) async-start(bf16[8,2,2,64,256]{4,3,2,1,0:T(8,128)(2,1)} %get-tuple-element.12), calls=%async_computation.1 | async-start | bytes 2097152 | tf_op jit(solution)/shard_map/all_to_all | solution.py:367
  35.7 12.5 %copy-start.3 = (f32[256]{0:T(256)S(1)}, f32[256]{0:T(256)}, u32[]{:S(2)}) copy-start(f32[256]{0:T(256)} %param.17) | copy-start | bytes 3076
  35.8 12.5 %copy-start.4 = (f32[256]{0:T(256)S(1)}, f32[256]{0:T(256)}, u32[]{:S(2)}) copy-start(f32[256]{0:T(256)} %param.19) | copy-start | bytes 3076
  44.7 21.9 %all-to-all-start = ((bf16[8,2,2,64,256]{4,3,2,1,0:T(8,128)(2,1)}), bf16[8,2,2,64,256]{4,3,2,1,0:T(8,128)(2,1)S(1)}, u32[]{:S(2)}, u32[]{:S(2)}) async-start(bf16[8,2,2,64,256]{4,3,2,1,0:T(8,128)(2,1)} %convs_outer.1), calls=%async_computation | async-start | bytes 2097152 | tf_op jit(solution)/shard_map/all_to_all | solution.py:367

commit v3 on v2

--- a/solution.py
+++ b/solution.py
@@ -47,14 +47,12 @@
     return copy
 
 
-def inner_body(info, inner, outer, halo, gain_one, w_one, gain_two, conv_two,
-               out, shared, s_one, s_two, w_two, kept, held, w_sem, kept_sems, sems):
+def inner_body(info, inner, outer, halo, gain_one, w_one, gain_two, w_two,
+               out, shared, s_one, s_two, kept, held, kept_sems, sems):
     frames, _, width, chans = inner.shape
     odd = info[0] == 1
     half_one = gain_one[...] * 0.5
     half_two = gain_two[...] * 0.5
-    load = pltpu.make_async_copy(conv_two, w_two, w_sem)
-    load.start()
 
     def put_first(frame, index):
         if index < HALF:
@@ -78,7 +76,6 @@
                 for ahead in range(index * 3 // 2, (index + 1) * 3 // 2):
                     put_first(frame + 1, ahead)
             put_second(frame, index)
-    load.wait()
     for frame in range(frames):
         here = slice(chans, 2 * chans)
         for index in range(HALF):
@@ -96,7 +93,7 @@
 
 
 def outer_body(info, outer, halo, shared, gain_one, w_one, gain_two, conv_two,
-               out, s_one, s_two_a, s_two_b, w_two, kept, held, w_sem, kept_sems, sems):
+               out, s_one, s_two_a, s_two_b, kept, w_two, held, kept_sems, w_sem, sems):
     frames, _, width, chans = outer.shape
     odd, goes_on = info[0] == 1, info[1] == 1
     new_at = jnp.where(odd, HALF, 0)
@@ -165,18 +162,18 @@
         outer_body if is_outer else inner_body,
         in_specs=[
             pl.BlockSpec(memory_space=pltpu.SMEM), here, here, there if is_outer else here,
-            here, here, here, there,
+            here, here, here, there if is_outer else here,
         ],
         out_specs=[there] if is_outer else [there, there],
         out_shape=[mixed] if is_outer else [mixed, keep],
         scratch_shapes=[
             stack(first_rows),
             *two,
-            pltpu.VMEM(conv_two.shape, BF16),
             pltpu.VMEM((frames, HALF, cols, chans), BF16),
+            *([pltpu.VMEM(conv_two.shape, BF16)] if is_outer else []),
             pltpu.VMEM((frames, HALF, owners, own, chans), BF16),
-            pltpu.SemaphoreType.DMA,
             pltpu.SemaphoreType.DMA((frames,)),
+            *([pltpu.SemaphoreType.DMA] if is_outer else []),
             pltpu.SemaphoreType.DMA((frames, HALF)),
         ],
         compiler_params=pltpu.CompilerParams(vmem_limit_bytes=28 * 1024 * 1024),
@@ -186,12 +183,11 @@
         name="convs_outer" if is_outer else "convs_inner",
     )(
         info, *((outer, halo, far(shared)) if is_outer else (inner, outer, halo)),
-        gain_one, near(conv_one), gain_two, far(conv_two),
-    )
-
-
-def attend_body(group, x_ref, gain_three, kernel, gain_four, wq, wk, wv, wo, *refs):
-    out_ref = refs[-1]
+        gain_one, near(conv_one), gain_two, far(conv_two) if is_outer else near(conv_two),
+    )
+
+
+def attend_body(group, order, x_ref, gain_three, kernel, gain_four, wq, wk, wv, wo, *refs):
     frames, pixels, chans = x_ref.shape
     count = frames * pixels
     half_three = gain_three[...] * 0.5
@@ -228,25 +224,32 @@
     final = timed + jnp.dot(
         attended.reshape(count, chans), wo[...], preferred_element_type=F32
     )
-    out_ref[...] = final.astype(BF16).reshape(frames, pixels, chans)
-
-
-def attend_chunk(x, weights, tile, group, result=None):
+    final = final.astype(BF16).reshape(frames, pixels, chans)
+    if len(refs) == 1:
+        refs[0][...] = final
+        return
+    *outs, held = refs
+    held[...] = final
+    share = frames // len(outs)
+    for n, out in enumerate(outs):
+        out[...] = held[pl.ds(order[n] * share, share)]
+
+
+def attend_chunk(x, order, weights, tile, group, members=0):
     frames, pixels, chans = x.shape
     tile = min(tile, pixels)
-    skip = 0 if result is None else pixels // tile
-    given = [] if result is None else [result]
-    far = lambda v: pltpu.with_memory_space_constraint(v, pltpu.HBM)
+    near = lambda v: pltpu.with_memory_space_constraint(v, pltpu.VMEM)
     whole = lambda a: pl.BlockSpec(a.shape, lambda p: (0,) * a.ndim)
-    return pl.pallas_call(
+    count, share = (members, frames // members) if members else (1, frames)
+    block = lambda depth: pl.BlockSpec((depth, tile, chans), lambda p: (0, p, 0))
+    result = pl.pallas_call(
         functools.partial(attend_body, group),
         grid=(pixels // tile,),
-        in_specs=[pl.BlockSpec((frames, tile, chans), lambda p: (0, p, 0))]
-        + [whole(w) for w in weights]
-        + [pl.BlockSpec(memory_space=pltpu.HBM)] * len(given),
-        out_specs=pl.BlockSpec((frames, tile, chans), lambda p: (0, p + skip, 0)),
-        out_shape=pltpu.HBM((frames, 2 * pixels, chans), BF16),
-        input_output_aliases={1 + len(weights): 0} if given else {},
+        in_specs=[pl.BlockSpec(memory_space=pltpu.SMEM), block(frames)]
+        + [whole(w) for w in weights],
+        out_specs=[block(share)] * count,
+        out_shape=[pltpu.HBM((share, pixels, chans), BF16)] * count,
+        scratch_shapes=[pltpu.VMEM((frames, tile, chans), BF16)] if members else [],
         compiler_params=pltpu.CompilerParams(vmem_limit_bytes=32 * 1024 * 1024),
         cost_estimate=pl.CostEstimate(
             flops=2 * frames * pixels * chans * chans * 9,
@@ -254,73 +257,71 @@
             transcendentals=0,
         ),
         name="attend",
-    )(x, *[w if w.shape[0] == 1 else far(w) for w in weights], *given)
-
-
-def place_body(starts, back, out, sems):
-    owners, _, parts, rows, own, _ = back.shape
-    copies = [
-        pltpu.make_async_copy(
-            back.at[o, :, n],
-            out.at[:, pl.ds(starts[n], rows), pl.ds(o * own, own)],
-            sems.at[n, o],
+    )(order, x, *[w if w.shape[0] == 1 else near(w) for w in weights])
+    return result if members else result[0]
+
+
+def place_body(count, where, *refs):
+    pieces, (out, sems) = refs[:count], refs[-2:]
+    if count == 1:
+        pieces = [(n, pieces[0].at[n]) for n in range(pieces[0].shape[0])]
+    else:
+        pieces = [(where[1 + n], piece) for n, piece in enumerate(pieces)]
+    rows, own = pieces[0][1].shape[1:3]
+    copies = []
+    for n, (member, piece) in enumerate(pieces):
+        columns = pl.ds(pl.multiple_of(member * own, own), own)
+        copies.append(
+            pltpu.make_async_copy(piece, out.at[:, pl.ds(where[0], rows), columns], sems.at[n])
         )
-        for o in range(owners)
-        for n in range(parts)
-    ]
     for copy in copies:
         copy.start()
     for copy in copies:
         copy.wait()
 
 
-def place(starts, back, shape):
-    owners, _, parts = back.shape[:3]
+def place(where, pieces, shape, result=None):
+    here = pl.BlockSpec(memory_space=pltpu.VMEM)
+    there = pl.BlockSpec(memory_space=pltpu.HBM)
+    scalars = pl.BlockSpec(memory_space=pltpu.SMEM)
+    given = [] if result is None else [result]
     return pl.pallas_call(
-        place_body,
-        in_specs=[
-            pl.BlockSpec(memory_space=pltpu.SMEM), pl.BlockSpec(memory_space=pltpu.VMEM),
-        ],
-        out_specs=pl.BlockSpec(memory_space=pltpu.HBM),
+        functools.partial(place_body, len(pieces)),
+        in_specs=[scalars] + [here] * len(pieces) + [there] * len(given),
+        out_specs=there,
         out_shape=pltpu.HBM(shape, BF16),
-        scratch_shapes=[pltpu.SemaphoreType.DMA((parts, owners))],
+        input_output_aliases={1 + len(pieces): 0} if given else {},
+        scratch_shapes=[pltpu.SemaphoreType.DMA((where.shape[0],))],
         compiler_params=pltpu.CompilerParams(vmem_limit_bytes=16 * 1024 * 1024),
         cost_estimate=pl.CostEstimate(
-            flops=0, bytes_accessed=4 * 1024 * 1024, transcendentals=0
+            flops=0, bytes_accessed=2 * 1024 * 1024, transcendentals=0
         ),
         name="place",
-    )(starts, back)
-
-
-def split_body(starts, video, inner, outer, sems):
-    copies = [
-        pltpu.make_async_copy(video.at[:, pl.ds(starts[n], HALF)], part, sems.at[n])
-        for n, part in ((1, outer), (0, inner))
-    ]
-    for copy in copies:
-        copy.start()
-    for copy in copies:
-        copy.wait()
-
-
-def split(starts, video):
+    )(where, *[pltpu.with_memory_space_constraint(v, pltpu.VMEM) for v in pieces], *given)
+
+
+def cut_body(start, video, part, sem):
+    copy = pltpu.make_async_copy(video.at[:, pl.ds(start[0], HALF)], part, sem)
+    copy.start()
+    copy.wait()
+
+
+def cut(start, video):
     frames, rows, cols, chans = video.shape
-    part = jax.ShapeDtypeStruct((frames, HALF, cols, chans), BF16)
-    here = pl.BlockSpec(memory_space=pltpu.VMEM)
     return pl.pallas_call(
-        split_body,
+        cut_body,
         in_specs=[
             pl.BlockSpec(memory_space=pltpu.SMEM), pl.BlockSpec(memory_space=pltpu.HBM),
         ],
-        out_specs=[here, here],
-        out_shape=[part, part],
-        scratch_shapes=[pltpu.SemaphoreType.DMA((2,))],
+        out_specs=pl.BlockSpec(memory_space=pltpu.VMEM),
+        out_shape=pltpu.VMEM((frames, HALF, cols, chans), BF16),
+        scratch_shapes=[pltpu.SemaphoreType.DMA],
         compiler_params=pltpu.CompilerParams(vmem_limit_bytes=8 * 1024 * 1024),
         cost_estimate=pl.CostEstimate(
-            flops=0, bytes_accessed=4 * 1024 * 1024, transcendentals=0
+            flops=0, bytes_accessed=2 * 1024 * 1024, transcendentals=0
         ),
-        name="split",
-    )(starts, pltpu.with_memory_space_constraint(video, pltpu.HBM))
+        name="cut",
+    )(start, pltpu.with_memory_space_constraint(video, pltpu.HBM))
 
 
 def shards(
@@ -356,20 +357,36 @@
         query_weight, key_weight, value_weight, out_weight,
     )
     starts = jnp.stack([inner_start, outer_start])
-    inner, outer = split(starts, video)
+    outer = cut(starts[1:], video)
     from_outer = lax.ppermute(outer, "strip", neighbours)
+    inner = cut(starts[:1], video)
     from_sibling = lax.ppermute(inner, "strip", siblings)
 
-    final = shared = None
-    for halo in (from_sibling, from_outer):
-        mixed, *kept = conv_chunk(info, inner, outer, halo, shared, owners, conv_weights)
-        shared = kept[0] if kept else None
-        block = lax.all_to_all(mixed, "tm", split_axis=0, concat_axis=0, tiled=True)
-        frames = block.shape[0] * block.shape[1]
-        final = attend_chunk(block.reshape(frames, -1, chans), attend_weights, 64, 16, final)
-    final = final.reshape(owners, block.shape[1], 2, *block.shape[2:])
-    back = lax.all_to_all(final, "tm", split_axis=0, concat_axis=0, tiled=True)
-    return place(starts, back, video.shape)
+    me = lax.axis_index("tm")
+    sides = owners // 2
+    steps = [(0, 0), (0, 1), (1, 0), (1, 1), (3, 0), (3, 1), (2, 1), (2, 0)]
+    member = lambda i, dy, dx: (i // 2 + dy) % sides * 2 + (i + dx) % 2
+    to = jnp.stack([member(me, dy, dx) for dy, dx in steps])
+    source = jnp.stack([member(me, sides - dy, dx) for dy, dx in steps])
+    exchange = lambda v: lax.all_to_all(v, "tm", split_axis=0, concat_axis=0, tiled=True)
+
+    mixed, shared = conv_chunk(info, inner, outer, from_sibling, None, owners, conv_weights)
+    block = exchange(mixed)
+    by_frame = (owners * block.shape[1], -1, chans)
+    final = attend_chunk(block.reshape(by_frame), to, attend_weights, 128, 16)
+    (mixed,) = conv_chunk(info, inner, outer, from_outer, shared, owners, conv_weights)
+    block = exchange(mixed)
+    finals = attend_chunk(block.reshape(by_frame), to, attend_weights, 128, 16, owners)
+    back = exchange(final.reshape(block.shape))
+    where = jnp.concatenate([starts[1:], source])
+    result = place(jnp.broadcast_to(starts[:1], where.shape), [back], video.shape)
+    backs = [finals[0]] + [
+        lax.ppermute(finals[n], "tm", [(i, member(i, dy, dx)) for i in range(owners)])
+        for n, (dy, dx) in enumerate(steps)
+        if n
+    ]
+    backs = [v.reshape(block.shape[1:]) for v in backs]
+    return place(where, backs, video.shape, result)
 
 
 def solution(mesh):

time: 109 us -> 103 us (0.945)
  blocking collectives: 32.5 us -> 0 us
  starting transfers between devices: 14.2 us -> 32.4 us
  waiting for transfers between devices: 19.7 us -> 29.8 us
  Pallas kernels: 41.9 us -> 38.2 us
  local copies, waits for them, and re-layouts: 0.02 us -> 1.51 us
    all_to_all x1 -> x0, blocking collectives: 32.5 us -> none  [shards(): back = lax.all_to_all(final, 'tm', split_axis=0, concat_axis=0, tiled=True)]
    ppermute x0 -> x7, starting transfers between devices: none -> 14.1 us  [shards(): lax.ppermute(finals[n], 'tm', [(i, member(i, dy, dx)) for i in range(owne...]
    ppermute x0 -> x7, waiting for transfers between devices: none -> 10.5 us  [shards(): lax.ppermute(finals[n], 'tm', [(i, member(i, dy, dx)) for i in range(owne...]
    all_to_all x2 -> x3, starting transfers between devices: 10.2 us -> 14.3 us  [shards(): lax.all_to_all(v, 'tm', split_axis=0, concat_axis=0, tiled=True)]
    pallas_call x2, Pallas kernels: 15.1 us -> 12 us  [attend_chunk(): pl.pallas_call(functools.partial(attend_body, group), grid=(pixels // til...]
    pallas_call x2, Pallas kernels: 22.7 us -> 20.4 us  [conv_chunk(): pl.pallas_call(outer_body if is_outer else inner_body, in_specs=[pl.Block...]
    pallas_call x2 -> x4, Pallas kernels: 4.08 us -> 5.7 us  [the longest x2 3.16 us: place(): pl.pallas_call(functools.partial(place_body, len(pieces)), in_specs=[scal...]
    unnamed x10 -> x24, local copies, waits for them, and re-layouts: 0.02 us -> 1.33 us
  transfers between devices with their start and end apart: 4 -> 12, of which waited for: 2 -> 6; matrix products, arithmetic and copies ran while one was open for 0% -> 0% of each run, Pallas kernels for 28% -> 34%
where the time goes in v3:
time: 103 us; the launch traced here: 102 us
  Pallas kernels  38.2 us (37%)
  starting transfers between devices  32.4 us (31%)
  waiting for transfers between devices  29.8 us (29%)
  local copies, waits for them, and re-layouts  1.51 us (1%)
    pallas_call x2, Pallas kernels, conv_chunk(): pl.pallas_call(outer_body if is_outer else inner_body, in_specs=[pl.Block...  20.4 us
    all_to_all x3, waiting for transfers between devices, shards(): lax.all_to_all(v, 'tm', split_axis=0, concat_axis=0, tiled=True)  19.3 us
    all_to_all x3, starting transfers between devices, shards(): lax.all_to_all(v, 'tm', split_axis=0, concat_axis=0, tiled=True)  14.3 us
    ppermute x7, starting transfers between devices, shards(): lax.ppermute(finals[n], 'tm', [(i, member(i, dy, dx)) for i in range(owne...  14.1 us
    pallas_call x2, Pallas kernels, attend_chunk(): pl.pallas_call(functools.partial(attend_body, group), grid=(pixels // til...  12 us
    ppermute x7, waiting for transfers between devices, shards(): lax.ppermute(finals[n], 'tm', [(i, member(i, dy, dx)) for i in range(owne...  10.5 us
    ppermute x1, starting transfers between devices, shards(): from_outer = lax.ppermute(outer, 'strip', neighbours)  3.87 us
    pallas_call x2, Pallas kernels, place(): pl.pallas_call(functools.partial(place_body, len(pieces)), in_specs=[scal...  3.16 us
  transfers between devices with their start and end apart: 12, of which 6 were waited for; matrix products, arithmetic and copies ran while one was open for 0% of the time, Pallas kernels for 34%

profile of v3, /device:TPU:160, one launch (start us, length us, event | category | flops | bytes accessed | tf_op | source)
XLA Modules:
  0.0 102.5 jit_solution(1857453815603615031)
XLA Ops:
  0.0 1.2 %cut.3.inner = bf16[2,2,512,256]{3,2,1,0:T(8,128)(2,1)S(1)} custom-call(s32[1]{0:T(128)} %bitcast.13.start, bf16[2,4,512,256]{3,2,1,0:T(8,128)(2,1)} %video.3), custom_call_target="tpu_custom_call" | custom-call | bytes 2097152 | tf_op jit(solution)/shard_map/cut/pallas_call | solution.py:311
  1.2 0.0 copy-start.1
  1.3 0.1 collective-permute-start.1
  1.4 1.3 %cut.2.outer = bf16[2,2,512,256]{3,2,1,0:T(8,128)(2,1)S(1)} custom-call(s32[1]{0:T(128)} %bitcast.start, bf16[2,4,512,256]{3,2,1,0:T(8,128)(2,1)} %video.3), custom_call_target="tpu_custom_call" | custom-call | bytes 2097152 | tf_op jit(solution)/shard_map/cut/pallas_call | solution.py:311
  2.7 3.9 %collective-permute-start = (bf16[2,2,512,256]{3,2,1,0:T(8,128)(2,1)S(1)}, bf16[2,2,512,256]{3,2,1,0:T(8,128)(2,1)}, u32[]{:S(2)}, u32[]{:S(2)}) collective-permute-start(bf16[2,2,512,256]{3,2,1,0:T(8,128)(2,1)S(1)} %cut.2.outer), channel_id=1, source_target_pairs={{1,2},{2,1},{3,4},{4,3},{5,6},{6,5},{7,8},{8,7},{9,10},{10,9},{11,... | collective-permute-start | bytes 3145736 | tf_op jit(solution)/shard_map/ppermute | solution.py:361
  6.6 0.1 pad_add_fusion.info
  6.7 0.0 copy-start.2
  6.7 1.3 %copy-done.2 = bf16[3,3,256,256]{3,2,1,0:T(8,128)(2,1)S(1)} copy-done((bf16[3,3,256,256]{3,2,1,0:T(8,128)(2,1)S(1)}, bf16[3,3,256,256]{3,2,1,0:T(8,128)(2,1)}, u32[]{:S(2)}) %copy-start.2) | copy-done | bytes 1179672
  8.0 10.9 %convs_inner.1 = (bf16[8,2,2,64,256]{4,3,2,1,0:T(8,128)(2,1)}, bf16[2,2,512,256]{3,2,1,0:T(8,128)(2,1)}) custom-call(s32[2]{0:T(128)S(1)} %pad_add_fusion.info, bf16[2,2,512,256]{3,2,1,0:T(8,128)(2,1)S(1)} %cut.3.inner, bf16[2,2,512,256]{3,2,1,0:T(8,128)(2,1)S(1)} %cut.2.outer, bf16[2,2,512,256]{3,2,1,0:T(8,128)(2,1)} %collective-permute-done.1.halo, ...), custom_call_target="tpu_custom_call" | custom-call | flops 7247757312 | bytes 8388608 | tf_op jit(solution)/shard_map/convs_inner/pallas_call | solution.py:161
  18.8 6.6 %all-to-all-start.1 = ((bf16[8,2,2,64,256]{4,3,2,1,0:T(8,128)(2,1)}), bf16[8,2,2,64,256]{4,3,2,1,0:T(8,128)(2,1)S(1)}, u32[]{:S(2)}, u32[]{:S(2)}) async-start(bf16[8,2,2,64,256]{4,3,2,1,0:T(8,128)(2,1)} %get-tuple-element.24), calls=%async_computation.1 | async-start | bytes 2097152 | tf_op jit(solution)/shard_map/all_to_all | solution.py:371
  25.5 9.5 %convs_outer.1 = bf16[8,2,2,64,256]{4,3,2,1,0:T(8,128)(2,1)} custom-call(s32[2]{0:T(128)S(1)} %pad_add_fusion.info, bf16[2,2,512,256]{3,2,1,0:T(8,128)(2,1)S(1)} %cut.2.outer, bf16[2,2,512,256]{3,2,1,0:T(8,128)(2,1)} %collective-permute-done.halo, bf16[2,2,512,256]{3,2,1,0:T(8,128)(2,1)} %get-tuple-element.15.shared, f32[1,256]{1,0:T(1,128)S(1)} %bitcast.49, ...), custom_call_target="tpu_custom_call" | custom-call | flops 4831838208 | bytes 8388608 | tf_op jit(solution)/shard_map/convs_outer/pallas_call | solution.py:161
  35.1 9.1 %all-to-all-done.1 = bf16[8,2,2,64,256]{4,3,2,1,0:T(8,128)(2,1)S(1)} async-done(((bf16[8,2,2,64,256]{4,3,2,1,0:T(8,128)(2,1)}), bf16[8,2,2,64,256]{4,3,2,1,0:T(8,128)(2,1)S(1)}, u32[]{:S(2)}, u32[]{:S(2)}) %all-to-all-start.1) | async-done | bytes 1048608 | tf_op jit(solution)/shard_map/all_to_all | solution.py:371
  44.2 3.6 %all-to-all-start = ((bf16[8,2,2,64,256]{4,3,2,1,0:T(8,128)(2,1)}), bf16[8,2,2,64,256]{4,3,2,1,0:T(8,128)(2,1)S(1)}, u32[]{:S(2)}, u32[]{:S(2)}) async-start(bf16[8,2,2,64,256]{4,3,2,1,0:T(8,128)(2,1)} %convs_outer.1), calls=%async_computation | async-start | bytes 2097152 | tf_op jit(solution)/shard_map/all_to_all | solution.py:371
  47.8 0.1 stack.68.order
  48.0 6.0 %attend.3 = bf16[16,128,256]{2,1,0:T(8,128)(2,1)} custom-call(s32[8]{0:T(128)S(1)} %stack.68.order, bf16[16,128,256]{2,1,0:T(8,128)(2,1)S(1)} %bitcast.33, f32[1,256]{1,0:T(1,128)S(1)} %bitcast.52, bf16[768,256]{1,0:T(8,128)(2,1)S(1)} %bitcast.46, f32[1,256]{1,0:T(1,128)S(1)} %bitcast.54, bf16[256,256]{1,0:T(8,128)(2,1)S(1)} %copy-done.4, ...), custom_call_target="tpu_custom_call" | custom-call | flops 2415919104 | bytes 4194304 | tf_op jit(solution)/shard_map/attend/pallas_call | solution.py:245
  54.0 10.3 %all-to-all-done = bf16[8,2,2,64,256]{4,3,2,1,0:T(8,128)(2,1)S(1)} async-done(((bf16[8,2,2,64,256]{4,3,2,1,0:T(8,128)(2,1)}), bf16[8,2,2,64,256]{4,3,2,1,0:T(8,128)(2,1)S(1)}, u32[]{:S(2)}, u32[]{:S(2)}) %all-to-all-start) | async-done | bytes 1048608 | tf_op jit(solution)/shard_map/all_to_all | solution.py:371
  64.2 4.1 %all-to-all-start.2 = ((bf16[8,2,2,64,256]{4,3,2,1,0:T(8,128)(2,1)}), bf16[8,2,2,64,256]{4,3,2,1,0:T(8,128)(2,1)S(1)}, u32[]{:S(2)}, u32[]{:S(2)}) async-start(bf16[8,2,2,64,256]{4,3,2,1,0:T(8,128)(2,1)} %bitcast.56), calls=%async_computation.2 | async-start | bytes 2097152 | tf_op jit(solution)/shard_map/all_to_all | solution.py:371
  68.3 6.0 %attend.2 = (bf16[2,128,256]{2,1,0:T(8,128)(2,1)}, bf16[2,128,256]{2,1,0:T(8,128)(2,1)}, bf16[2,128,256]{2,1,0:T(8,128)(2,1)}, bf16[2,128,256]{2,1,0:T(8,128)(2,...) custom-call(s32[8]{0:T(128)S(1)} %stack.68.order, ...), custom_call_target="tpu_custom_call" | custom-call | flops 2415919104 | bytes 4194304 | tf_op jit(solution)/shard_map/attend/pallas_call | solution.py:245
  74.4 3.5 %collective-permute-start.2 = (bf16[2,128,256]{2,1,0:T(8,128)(2,1)}, bf16[2,128,256]{2,1,0:T(8,128)(2,1)S(1)}, u32[]{:S(2)}, u32[]{:S(2)}) collective-permute-start(bf16[2,128,256]{2,1,0:T(8,128)(2,1)} %get-tuple-element.17), channel_id=1, source_target_pairs={{0,32},{32,0},{64,96},{96,64},{128,160},{160,128},{192,224},{224,1... | collective-permute-start | bytes 393224 | tf_op jit(solution)/shard_map/ppermute | solution.py:384
  77.9 1.5 %collective-permute-start.3 = (bf16[2,128,256]{2,1,0:T(8,128)(2,1)}, bf16[2,128,256]{2,1,0:T(8,128)(2,1)S(1)}, u32[]{:S(2)}, u32[]{:S(2)}) collective-permute-start(bf16[2,128,256]{2,1,0:T(8,128)(2,1)} %get-tuple-element.18), channel_id=1, source_target_pairs={{0,64},{32,96},{64,128},{96,160},{128,192},{160,224},{192,0},{224,... | collective-permute-start | bytes 393224 | tf_op jit(solution)/shard_map/ppermute | solution.py:384
  79.4 1.5 %collective-permute-start.4 = (bf16[2,128,256]{2,1,0:T(8,128)(2,1)}, bf16[2,128,256]{2,1,0:T(8,128)(2,1)S(1)}, u32[]{:S(2)}, u32[]{:S(2)}) collective-permute-start(bf16[2,128,256]{2,1,0:T(8,128)(2,1)} %get-tuple-element.19), channel_id=1, source_target_pairs={{0,96},{32,64},{64,160},{96,128},{128,224},{160,192},{192,32},{224... | collective-permute-start | bytes 393224 | tf_op jit(solution)/shard_map/ppermute | solution.py:384
  80.8 1.8 %collective-permute-start.5 = (bf16[2,128,256]{2,1,0:T(8,128)(2,1)}, bf16[2,128,256]{2,1,0:T(8,128)(2,1)S(1)}, u32[]{:S(2)}, u32[]{:S(2)}) collective-permute-start(bf16[2,128,256]{2,1,0:T(8,128)(2,1)} %get-tuple-element.20), channel_id=1, source_target_pairs={{0,192},{32,224},{64,0},{96,32},{128,64},{160,96},{192,128},{224,1... | collective-permute-start | bytes 393224 | tf_op jit(solution)/shard_map/ppermute | solution.py:384
  82.6 3.0 %collective-permute-start.6 = (bf16[2,128,256]{2,1,0:T(8,128)(2,1)}, bf16[2,128,256]{2,1,0:T(8,128)(2,1)S(1)}, u32[]{:S(2)}, u32[]{:S(2)}) collective-permute-start(bf16[2,128,256]{2,1,0:T(8,128)(2,1)} %get-tuple-element.21), channel_id=1, source_target_pairs={{0,224},{32,192},{64,32},{96,0},{128,96},{160,64},{192,160},{224,1... | collective-permute-start | bytes 393224 | tf_op jit(solution)/shard_map/ppermute | solution.py:384
  85.6 2.2 %collective-permute-done.2 = bf16[2,128,256]{2,1,0:T(8,128)(2,1)S(1)} collective-permute-done((bf16[2,128,256]{2,1,0:T(8,128)(2,1)}, bf16[2,128,256]{2,1,0:T(8,128)(2,1)S(1)}, u32[]{:S(2)}, u32[]{:S(2)}) %collective-permute-start.2) | collective-permute-done | bytes 131104 | tf_op jit(solution)/shard_map/ppermute | solution.py:384
  87.7 2.7 %collective-permute-start.7 = (bf16[2,128,256]{2,1,0:T(8,128)(2,1)}, bf16[2,128,256]{2,1,0:T(8,128)(2,1)S(1)}, u32[]{:S(2)}, u32[]{:S(2)}) collective-permute-start(bf16[2,128,256]{2,1,0:T(8,128)(2,1)} %get-tuple-element.22), channel_id=1, source_target_pairs={{0,160},{32,128},{64,224},{96,192},{128,32},{160,0},{192,96},{224,... | collective-permute-start | bytes 393224 | tf_op jit(solution)/shard_map/ppermute | solution.py:384
  90.4 0.3 collective-permute-start.8
  90.7 0.1 concatenate.3.where
  90.8 1.6 %place.2.refs_8_ = bf16[2,4,512,256]{3,2,1,0:T(8,128)(2,1)} custom-call(s32[9]{0:T(128)S(1)} %broadcast_in_dim.2.where, bf16[8,2,2,64,256]{4,3,2,1,0:T(8,128)(2,1)S(1)} %all-to-all-done.2.refs_0_), custom_call_target="tpu_custom_call" | custom-call | bytes 2097152 | tf_op jit(solution)/shard_map/place/pallas_call | solution.py:288
  92.4 1.6 %collective-permute-done.6 = bf16[2,128,256]{2,1,0:T(8,128)(2,1)S(1)} collective-permute-done((bf16[2,128,256]{2,1,0:T(8,128)(2,1)}, bf16[2,128,256]{2,1,0:T(8,128)(2,1)S(1)}, u32[]{:S(2)}, u32[]{:S(2)}) %collective-permute-start.6) | collective-permute-done | bytes 131104 | tf_op jit(solution)/shard_map/ppermute | solution.py:384
  94.0 4.7 %collective-permute-done.7 = bf16[2,128,256]{2,1,0:T(8,128)(2,1)S(1)} collective-permute-done((bf16[2,128,256]{2,1,0:T(8,128)(2,1)}, bf16[2,128,256]{2,1,0:T(8,128)(2,1)S(1)}, u32[]{:S(2)}, u32[]{:S(2)}) %collective-permute-start.7) | collective-permute-done | bytes 131104 | tf_op jit(solution)/shard_map/ppermute | solution.py:384
  98.6 2.1 %collective-permute-done.8 = bf16[2,128,256]{2,1,0:T(8,128)(2,1)S(1)} collective-permute-done((bf16[2,128,256]{2,1,0:T(8,128)(2,1)}, bf16[2,128,256]{2,1,0:T(8,128)(2,1)S(1)}, u32[]{:S(2)}, u32[]{:S(2)}) %collective-permute-start.8) | collective-permute-done | bytes 131104 | tf_op jit(solution)/shard_map/ppermute | solution.py:384
  100.7 1.6 %place.3 = bf16[2,4,512,256]{3,2,1,0:T(8,128)(2,1)} custom-call(s32[9]{0:T(128)S(1)} %concatenate.3.where, bf16[2,2,64,256]{3,2,1,0:T(8,128)(2,1)S(1)} %bitcast.34, bf16[2,2,64,256]{3,2,1,0:T(8,128)(2,1)S(1)} %bitcast.35, bf16[2,2,64,256]{3,2,1,0:T(8,128)(2,1)S(1)} %bitcast.36, bf16[2,2,64,256]{3,2,1,0:T(8,128)(2,1)S(1)} %bitcast.37, ...), custom_call_target="tpu_custom_call", output_to_operand_aliasing={{}: (9, {})} | custom-call | bytes 2097152 | tf_op jit(solution)/shard_map/place/pallas_call | solution.py:288
  (28 shorter events, 0.1 us)
Async XLA Ops:
  1.2 5.4 %copy-start.1 = (bf16[3,3,256,256]{3,2,1,0:T(8,128)(2,1)S(1)}, bf16[3,3,256,256]{3,2,1,0:T(8,128)(2,1)}, u32[]{:S(2)}) copy-start(bf16[3,3,256,256]{3,2,1,0:T(8,128)(2,1)} %param.14) | copy-start | bytes 3538948
  1.3 5.4 %copy-start.8 = (f32[256]{0:T(256)S(1)}, f32[256]{0:T(256)}, u32[]{:S(2)}) copy-start(f32[256]{0:T(256)} %param.13) | copy-start | bytes 3076
  1.3 5.4 %copy-start.9 = (f32[256]{0:T(256)S(1)}, f32[256]{0:T(256)}, u32[]{:S(2)}) copy-start(f32[256]{0:T(256)} %param.15) | copy-start | bytes 3076
  1.3 5.4 %collective-permute-start.1 = (bf16[2,2,512,256]{3,2,1,0:T(8,128)(2,1)S(1)}, bf16[2,2,512,256]{3,2,1,0:T(8,128)(2,1)}, u32[]{:S(2)}, u32[]{:S(2)}) collective-permute-start(bf16[2,2,512,256]{3,2,1,0:T(8,128)(2,1)S(1)} %cut.3.inner), channel_id=1, source_target_pairs={{0,1},{1,0},{2,3},{3,2},{4,5},{5,4},{6,7},{7,6},{8,9},{9,8},{10,11... | collective-permute-start | bytes 3145736 | tf_op jit(solution)/shard_map/ppermute | solution.py:363
  2.7 22.8 %collective-permute-start = (bf16[2,2,512,256]{3,2,1,0:T(8,128)(2,1)S(1)}, bf16[2,2,512,256]{3,2,1,0:T(8,128)(2,1)}, u32[]{:S(2)}, u32[]{:S(2)}) collective-permute-start(bf16[2,2,512,256]{3,2,1,0:T(8,128)(2,1)S(1)} %cut.2.outer), channel_id=1, source_target_pairs={{1,2},{2,1},{3,4},{4,3},{5,6},{6,5},{7,8},{8,7},{9,10},{10,9},{11,... | collective-permute-start | bytes 3145736 | tf_op jit(solution)/shard_map/ppermute | solution.py:361
  6.7 1.3 %copy-start.2 = (bf16[3,3,256,256]{3,2,1,0:T(8,128)(2,1)S(1)}, bf16[3,3,256,256]{3,2,1,0:T(8,128)(2,1)}, u32[]{:S(2)}) copy-start(bf16[3,3,256,256]{3,2,1,0:T(8,128)(2,1)} %param.16) | copy-start | bytes 3538948
  18.8 25.3 %all-to-all-start.1 = ((bf16[8,2,2,64,256]{4,3,2,1,0:T(8,128)(2,1)}), bf16[8,2,2,64,256]{4,3,2,1,0:T(8,128)(2,1)S(1)}, u32[]{:S(2)}, u32[]{:S(2)}) async-start(bf16[8,2,2,64,256]{4,3,2,1,0:T(8,128)(2,1)} %get-tuple-element.24), calls=%async_computation.1 | async-start | bytes 2097152 | tf_op jit(solution)/shard_map/all_to_all | solution.py:371
  35.0 12.9 %copy-start.3 = (bf16[3,256,256]{2,1,0:T(8,128)(2,1)S(1)}, bf16[3,256,256]{2,1,0:T(8,128)(2,1)}, u32[]{:S(2)}) copy-start(bf16[3,256,256]{2,1,0:T(8,128)(2,1)} %param.18) | copy-start | bytes 1179652
  35.0 12.9 %copy-start.4 = (bf16[256,256]{1,0:T(8,128)(2,1)S(1)}, bf16[256,256]{1,0:T(8,128)(2,1)}, u32[]{:S(2)}) copy-start(bf16[256,256]{1,0:T(8,128)(2,1)} %wq.3) | copy-start | bytes 393220
  35.1 12.9 %copy-start.5 = (bf16[256,256]{1,0:T(8,128)(2,1)S(1)}, bf16[256,256]{1,0:T(8,128)(2,1)}, u32[]{:S(2)}) copy-start(bf16[256,256]{1,0:T(8,128)(2,1)} %wk.3) | copy-start | bytes 393220
  35.1 12.9 %copy-start.6 = (bf16[256,256]{1,0:T(8,128)(2,1)S(1)}, bf16[256,256]{1,0:T(8,128)(2,1)}, u32[]{:S(2)}) copy-start(bf16[256,256]{1,0:T(8,128)(2,1)} %wv.3) | copy-start | bytes 393220
  35.1 12.9 %copy-start.7 = (bf16[256,256]{1,0:T(8,128)(2,1)S(1)}, bf16[256,256]{1,0:T(8,128)(2,1)}, u32[]{:S(2)}) copy-start(bf16[256,256]{1,0:T(8,128)(2,1)} %wo.3) | copy-start | bytes 393220
  35.1 12.9 %copy-start.10 = (f32[256]{0:T(256)S(1)}, f32[256]{0:T(256)}, u32[]{:S(2)}) copy-start(f32[256]{0:T(256)} %param.17) | copy-start | bytes 3076
  35.1 12.9 %copy-start.11 = (f32[256]{0:T(256)S(1)}, f32[256]{0:T(256)}, u32[]{:S(2)}) copy-start(f32[256]{0:T(256)} %param.19) | copy-start | bytes 3076
  44.2 20.1 %all-to-all-start = ((bf16[8,2,2,64,256]{4,3,2,1,0:T(8,128)(2,1)}), bf16[8,2,2,64,256]{4,3,2,1,0:T(8,128)(2,1)S(1)}, u32[]{:S(2)}, u32[]{:S(2)}) async-start(bf16[8,2,2,64,256]{4,3,2,1,0:T(8,128)(2,1)} %convs_outer.1), calls=%async_computation | async-start | bytes 2097152 | tf_op jit(solution)/shard_map/all_to_all | solution.py:371
  64.2 26.5 %all-to-all-start.2 = ((bf16[8,2,2,64,256]{4,3,2,1,0:T(8,128)(2,1)}), bf16[8,2,2,64,256]{4,3,2,1,0:T(8,128)(2,1)S(1)}, u32[]{:S(2)}, u32[]{:S(2)}) async-start(bf16[8,2,2,64,256]{4,3,2,1,0:T(8,128)(2,1)} %bitcast.56), calls=%async_computation.2 | async-start | bytes 2097152 | tf_op jit(solution)/shard_map/all_to_all | solution.py:371
  74.4 26.3 %copy-start = (bf16[2,128,256]{2,1,0:T(8,128)(2,1)S(1)}, bf16[2,128,256]{2,1,0:T(8,128)(2,1)}, u32[]{:S(2)}) copy-start(bf16[2,128,256]{2,1,0:T(8,128)(2,1)} %get-tuple-element.16) | copy-start | bytes 393220
  74.4 13.4 %collective-permute-start.2 = (bf16[2,128,256]{2,1,0:T(8,128)(2,1)}, bf16[2,128,256]{2,1,0:T(8,128)(2,1)S(1)}, u32[]{:S(2)}, u32[]{:S(2)}) collective-permute-start(bf16[2,128,256]{2,1,0:T(8,128)(2,1)} %get-tuple-element.17), channel_id=1, source_target_pairs={{0,32},{32,0},{64,96},{96,64},{128,160},{160,128},{192,224},{224,1... | collective-permute-start | bytes 393224 | tf_op jit(solution)/shard_map/ppermute | solution.py:384
  77.9 12.5 %collective-permute-start.3 = (bf16[2,128,256]{2,1,0:T(8,128)(2,1)}, bf16[2,128,256]{2,1,0:T(8,128)(2,1)S(1)}, u32[]{:S(2)}, u32[]{:S(2)}) collective-permute-start(bf16[2,128,256]{2,1,0:T(8,128)(2,1)} %get-tuple-element.18), channel_id=1, source_target_pairs={{0,64},{32,96},{64,128},{96,160},{128,192},{160,224},{192,0},{224,... | collective-permute-start | bytes 393224 | tf_op jit(solution)/shard_map/ppermute | solution.py:384
  79.4 13.0 %collective-permute-start.4 = (bf16[2,128,256]{2,1,0:T(8,128)(2,1)}, bf16[2,128,256]{2,1,0:T(8,128)(2,1)S(1)}, u32[]{:S(2)}, u32[]{:S(2)}) collective-permute-start(bf16[2,128,256]{2,1,0:T(8,128)(2,1)} %get-tuple-element.19), channel_id=1, source_target_pairs={{0,96},{32,64},{64,160},{96,128},{128,224},{160,192},{192,32},{224... | collective-permute-start | bytes 393224 | tf_op jit(solution)/shard_map/ppermute | solution.py:384
  80.8 11.6 %collective-permute-start.5 = (bf16[2,128,256]{2,1,0:T(8,128)(2,1)}, bf16[2,128,256]{2,1,0:T(8,128)(2,1)S(1)}, u32[]{:S(2)}, u32[]{:S(2)}) collective-permute-start(bf16[2,128,256]{2,1,0:T(8,128)(2,1)} %get-tuple-element.20), channel_id=1, source_target_pairs={{0,192},{32,224},{64,0},{96,32},{128,64},{160,96},{192,128},{224,1... | collective-permute-start | bytes 393224 | tf_op jit(solution)/shard_map/ppermute | solution.py:384
  82.6 11.4 %collective-permute-start.6 = (bf16[2,128,256]{2,1,0:T(8,128)(2,1)}, bf16[2,128,256]{2,1,0:T(8,128)(2,1)S(1)}, u32[]{:S(2)}, u32[]{:S(2)}) collective-permute-start(bf16[2,128,256]{2,1,0:T(8,128)(2,1)} %get-tuple-element.21), channel_id=1, source_target_pairs={{0,224},{32,192},{64,32},{96,0},{128,96},{160,64},{192,160},{224,1... | collective-permute-start | bytes 393224 | tf_op jit(solution)/shard_map/ppermute | solution.py:384
  87.7 10.9 %collective-permute-start.7 = (bf16[2,128,256]{2,1,0:T(8,128)(2,1)}, bf16[2,128,256]{2,1,0:T(8,128)(2,1)S(1)}, u32[]{:S(2)}, u32[]{:S(2)}) collective-permute-start(bf16[2,128,256]{2,1,0:T(8,128)(2,1)} %get-tuple-element.22), channel_id=1, source_target_pairs={{0,160},{32,128},{64,224},{96,192},{128,32},{160,0},{192,96},{224,... | collective-permute-start | bytes 393224 | tf_op jit(solution)/shard_map/ppermute | solution.py:384
  90.4 10.3 %collective-permute-start.8 = (bf16[2,128,256]{2,1,0:T(8,128)(2,1)}, bf16[2,128,256]{2,1,0:T(8,128)(2,1)S(1)}, u32[]{:S(2)}, u32[]{:S(2)}) collective-permute-start(bf16[2,128,256]{2,1,0:T(8,128)(2,1)} %get-tuple-element.23), channel_id=1, source_target_pairs={{0,128},{32,160},{64,192},{96,224},{128,0},{160,32},{192,64},{224,... | collective-permute-start | bytes 393224 | tf_op jit(solution)/shard_map/ppermute | solution.py:384

commit v4 on v3

--- a/solution.py
+++ b/solution.py
@@ -364,7 +364,7 @@
 
     me = lax.axis_index("tm")
     sides = owners // 2
-    steps = [(0, 0), (0, 1), (1, 0), (1, 1), (3, 0), (3, 1), (2, 1), (2, 0)]
+    steps = [(0, 0), (2, 1), (1, 1), (3, 1), (2, 0), (0, 1), (1, 0), (3, 0)]
     member = lambda i, dy, dx: (i // 2 + dy) % sides * 2 + (i + dx) % 2
     to = jnp.stack([member(me, dy, dx) for dy, dx in steps])
     source = jnp.stack([member(me, sides - dy, dx) for dy, dx in steps])

time: 103 us -> 101 us (0.981)
  starting transfers between devices: 32.4 us -> 31 us
    ppermute x7, starting transfers between devices: 14.1 us -> 12.8 us  [shards(): lax.ppermute(finals[n], 'tm', [(i, member(i, dy, dx)) for i in range(owne...]
  transfers between devices with their start and end apart: 12 -> 12, of which waited for: 6 -> 7; matrix products, arithmetic and copies ran while one was open for 0% -> 0% of each run, Pallas kernels for 34% -> 35%
where the time goes in v4:
time: 101 us
  Pallas kernels  38.2 us (38%)
  starting transfers between devices  31 us (31%)
  waiting for transfers between devices  29.3 us (29%)
  local copies, waits for them, and re-layouts  1.51 us (1%)
    pallas_call x2, Pallas kernels, conv_chunk(): pl.pallas_call(outer_body if is_outer else inner_body, in_specs=[pl.Block...  20.4 us
    all_to_all x3, waiting for transfers between devices, shards(): lax.all_to_all(v, 'tm', split_axis=0, concat_axis=0, tiled=True)  19.3 us
    all_to_all x3, starting transfers between devices, shards(): lax.all_to_all(v, 'tm', split_axis=0, concat_axis=0, tiled=True)  14.3 us
    ppermute x7, starting transfers between devices, shards(): lax.ppermute(finals[n], 'tm', [(i, member(i, dy, dx)) for i in range(owne...  12.8 us
    pallas_call x2, Pallas kernels, attend_chunk(): pl.pallas_call(functools.partial(attend_body, group), grid=(pixels // til...  12 us
    ppermute x7, waiting for transfers between devices, shards(): lax.ppermute(finals[n], 'tm', [(i, member(i, dy, dx)) for i in range(owne...  9.94 us
    ppermute x1, starting transfers between devices, shards(): from_outer = lax.ppermute(outer, 'strip', neighbours)  3.87 us
    pallas_call x2, Pallas kernels, place(): pl.pallas_call(functools.partial(place_body, len(pieces)), in_specs=[scal...  3.16 us
  transfers between devices with their start and end apart: 12, of which 7 were waited for; matrix products, arithmetic and copies ran while one was open for 0% of the time, Pallas kernels for 35%

profile of v4, /device:TPU:160, one launch (start us, length us, event | category | flops | bytes accessed | tf_op | source)
XLA Modules:
  0.0 100.6 jit_solution(4743704497012832514)
XLA Ops:
  0.0 1.2 %cut.3.inner = bf16[2,2,512,256]{3,2,1,0:T(8,128)(2,1)S(1)} custom-call(s32[1]{0:T(128)} %bitcast.13.start, bf16[2,4,512,256]{3,2,1,0:T(8,128)(2,1)} %video.3), custom_call_target="tpu_custom_call" | custom-call | bytes 2097152 | tf_op jit(solution)/shard_map/cut/pallas_call | solution.py:311
  1.2 0.0 copy-start.1
  1.3 0.1 collective-permute-start.1
  1.4 1.3 %cut.2.outer = bf16[2,2,512,256]{3,2,1,0:T(8,128)(2,1)S(1)} custom-call(s32[1]{0:T(128)} %bitcast.start, bf16[2,4,512,256]{3,2,1,0:T(8,128)(2,1)} %video.3), custom_call_target="tpu_custom_call" | custom-call | bytes 2097152 | tf_op jit(solution)/shard_map/cut/pallas_call | solution.py:311
  2.7 3.9 %collective-permute-start = (bf16[2,2,512,256]{3,2,1,0:T(8,128)(2,1)S(1)}, bf16[2,2,512,256]{3,2,1,0:T(8,128)(2,1)}, u32[]{:S(2)}, u32[]{:S(2)}) collective-permute-start(bf16[2,2,512,256]{3,2,1,0:T(8,128)(2,1)S(1)} %cut.2.outer), channel_id=1, source_target_pairs={{1,2},{2,1},{3,4},{4,3},{5,6},{6,5},{7,8},{8,7},{9,10},{10,9},{11,... | collective-permute-start | bytes 3145736 | tf_op jit(solution)/shard_map/ppermute | solution.py:361
  6.6 0.1 pad_add_fusion.info
  6.7 0.0 copy-start.2
  6.7 1.3 %copy-done.2 = bf16[3,3,256,256]{3,2,1,0:T(8,128)(2,1)S(1)} copy-done((bf16[3,3,256,256]{3,2,1,0:T(8,128)(2,1)S(1)}, bf16[3,3,256,256]{3,2,1,0:T(8,128)(2,1)}, u32[]{:S(2)}) %copy-start.2) | copy-done | bytes 1179672
  8.0 10.9 %convs_inner.1 = (bf16[8,2,2,64,256]{4,3,2,1,0:T(8,128)(2,1)}, bf16[2,2,512,256]{3,2,1,0:T(8,128)(2,1)}) custom-call(s32[2]{0:T(128)S(1)} %pad_add_fusion.info, bf16[2,2,512,256]{3,2,1,0:T(8,128)(2,1)S(1)} %cut.3.inner, bf16[2,2,512,256]{3,2,1,0:T(8,128)(2,1)S(1)} %cut.2.outer, bf16[2,2,512,256]{3,2,1,0:T(8,128)(2,1)} %collective-permute-done.1.halo, ...), custom_call_target="tpu_custom_call" | custom-call | flops 7247757312 | bytes 8388608 | tf_op jit(solution)/shard_map/convs_inner/pallas_call | solution.py:161
  18.8 6.6 %all-to-all-start.1 = ((bf16[8,2,2,64,256]{4,3,2,1,0:T(8,128)(2,1)}), bf16[8,2,2,64,256]{4,3,2,1,0:T(8,128)(2,1)S(1)}, u32[]{:S(2)}, u32[]{:S(2)}) async-start(bf16[8,2,2,64,256]{4,3,2,1,0:T(8,128)(2,1)} %get-tuple-element.24), calls=%async_computation.1 | async-start | bytes 2097152 | tf_op jit(solution)/shard_map/all_to_all | solution.py:371
  25.5 9.5 %convs_outer.1 = bf16[8,2,2,64,256]{4,3,2,1,0:T(8,128)(2,1)} custom-call(s32[2]{0:T(128)S(1)} %pad_add_fusion.info, bf16[2,2,512,256]{3,2,1,0:T(8,128)(2,1)S(1)} %cut.2.outer, bf16[2,2,512,256]{3,2,1,0:T(8,128)(2,1)} %collective-permute-done.halo, bf16[2,2,512,256]{3,2,1,0:T(8,128)(2,1)} %get-tuple-element.15.shared, f32[1,256]{1,0:T(1,128)S(1)} %bitcast.49, ...), custom_call_target="tpu_custom_call" | custom-call | flops 4831838208 | bytes 8388608 | tf_op jit(solution)/shard_map/convs_outer/pallas_call | solution.py:161
  35.1 9.1 %all-to-all-done.1 = bf16[8,2,2,64,256]{4,3,2,1,0:T(8,128)(2,1)S(1)} async-done(((bf16[8,2,2,64,256]{4,3,2,1,0:T(8,128)(2,1)}), bf16[8,2,2,64,256]{4,3,2,1,0:T(8,128)(2,1)S(1)}, u32[]{:S(2)}, u32[]{:S(2)}) %all-to-all-start.1) | async-done | bytes 1048608 | tf_op jit(solution)/shard_map/all_to_all | solution.py:371
  44.2 3.6 %all-to-all-start = ((bf16[8,2,2,64,256]{4,3,2,1,0:T(8,128)(2,1)}), bf16[8,2,2,64,256]{4,3,2,1,0:T(8,128)(2,1)S(1)}, u32[]{:S(2)}, u32[]{:S(2)}) async-start(bf16[8,2,2,64,256]{4,3,2,1,0:T(8,128)(2,1)} %convs_outer.1), calls=%async_computation | async-start | bytes 2097152 | tf_op jit(solution)/shard_map/all_to_all | solution.py:371
  47.8 0.1 stack.68.order
  48.0 6.0 %attend.3 = bf16[16,128,256]{2,1,0:T(8,128)(2,1)} custom-call(s32[8]{0:T(128)S(1)} %stack.68.order, bf16[16,128,256]{2,1,0:T(8,128)(2,1)S(1)} %bitcast.33, f32[1,256]{1,0:T(1,128)S(1)} %bitcast.52, bf16[768,256]{1,0:T(8,128)(2,1)S(1)} %bitcast.46, f32[1,256]{1,0:T(1,128)S(1)} %bitcast.54, bf16[256,256]{1,0:T(8,128)(2,1)S(1)} %copy-done.4, ...), custom_call_target="tpu_custom_call" | custom-call | flops 2415919104 | bytes 4194304 | tf_op jit(solution)/shard_map/attend/pallas_call | solution.py:245
  54.0 10.3 %all-to-all-done = bf16[8,2,2,64,256]{4,3,2,1,0:T(8,128)(2,1)S(1)} async-done(((bf16[8,2,2,64,256]{4,3,2,1,0:T(8,128)(2,1)}), bf16[8,2,2,64,256]{4,3,2,1,0:T(8,128)(2,1)S(1)}, u32[]{:S(2)}, u32[]{:S(2)}) %all-to-all-start) | async-done | bytes 1048608 | tf_op jit(solution)/shard_map/all_to_all | solution.py:371
  64.2 4.1 %all-to-all-start.2 = ((bf16[8,2,2,64,256]{4,3,2,1,0:T(8,128)(2,1)}), bf16[8,2,2,64,256]{4,3,2,1,0:T(8,128)(2,1)S(1)}, u32[]{:S(2)}, u32[]{:S(2)}) async-start(bf16[8,2,2,64,256]{4,3,2,1,0:T(8,128)(2,1)} %bitcast.56), calls=%async_computation.2 | async-start | bytes 2097152 | tf_op jit(solution)/shard_map/all_to_all | solution.py:371
  68.3 6.0 %attend.2 = (bf16[2,128,256]{2,1,0:T(8,128)(2,1)}, bf16[2,128,256]{2,1,0:T(8,128)(2,1)}, bf16[2,128,256]{2,1,0:T(8,128)(2,1)}, bf16[2,128,256]{2,1,0:T(8,128)(2,...) custom-call(s32[8]{0:T(128)S(1)} %stack.68.order, ...), custom_call_target="tpu_custom_call" | custom-call | flops 2415919104 | bytes 4194304 | tf_op jit(solution)/shard_map/attend/pallas_call | solution.py:245
  74.4 5.9 %collective-permute-start.2 = (bf16[2,128,256]{2,1,0:T(8,128)(2,1)}, bf16[2,128,256]{2,1,0:T(8,128)(2,1)S(1)}, u32[]{:S(2)}, u32[]{:S(2)}) collective-permute-start(bf16[2,128,256]{2,1,0:T(8,128)(2,1)} %get-tuple-element.17), channel_id=1, source_target_pairs={{0,160},{32,128},{64,224},{96,192},{128,32},{160,0},{192,96},{224,... | collective-permute-start | bytes 393224 | tf_op jit(solution)/shard_map/ppermute | solution.py:384
  80.3 0.6 collective-permute-start.3
  80.9 5.1 %collective-permute-start.4 = (bf16[2,128,256]{2,1,0:T(8,128)(2,1)}, bf16[2,128,256]{2,1,0:T(8,128)(2,1)S(1)}, u32[]{:S(2)}, u32[]{:S(2)}) collective-permute-start(bf16[2,128,256]{2,1,0:T(8,128)(2,1)} %get-tuple-element.19), channel_id=1, source_target_pairs={{0,224},{32,192},{64,32},{96,0},{128,96},{160,64},{192,160},{224,1... | collective-permute-start | bytes 393224 | tf_op jit(solution)/shard_map/ppermute | solution.py:384
  85.9 0.6 collective-permute-start.6
  86.5 3.9 %collective-permute-done.2 = bf16[2,128,256]{2,1,0:T(8,128)(2,1)S(1)} collective-permute-done((bf16[2,128,256]{2,1,0:T(8,128)(2,1)}, bf16[2,128,256]{2,1,0:T(8,128)(2,1)S(1)}, u32[]{:S(2)}, u32[]{:S(2)}) %collective-permute-start.2) | collective-permute-done | bytes 131104 | tf_op jit(solution)/shard_map/ppermute | solution.py:384
  90.4 0.0 collective-permute-start.7
  90.4 2.6 %collective-permute-done.3 = bf16[2,128,256]{2,1,0:T(8,128)(2,1)S(1)} collective-permute-done((bf16[2,128,256]{2,1,0:T(8,128)(2,1)}, bf16[2,128,256]{2,1,0:T(8,128)(2,1)S(1)}, u32[]{:S(2)}, u32[]{:S(2)}) %collective-permute-start.3) | collective-permute-done | bytes 131104 | tf_op jit(solution)/shard_map/ppermute | solution.py:384
  93.0 0.6 collective-permute-start.8
  93.6 0.1 concatenate.3.where
  93.7 1.6 %place.2.refs_8_ = bf16[2,4,512,256]{3,2,1,0:T(8,128)(2,1)} custom-call(s32[9]{0:T(128)S(1)} %broadcast_in_dim.2.where, bf16[8,2,2,64,256]{4,3,2,1,0:T(8,128)(2,1)S(1)} %all-to-all-done.2.refs_0_), custom_call_target="tpu_custom_call" | custom-call | bytes 2097152 | tf_op jit(solution)/shard_map/place/pallas_call | solution.py:288
  95.3 0.8 collective-permute-done.5
  96.1 0.3 collective-permute-done.6
  96.4 2.4 %collective-permute-done.7 = bf16[2,128,256]{2,1,0:T(8,128)(2,1)S(1)} collective-permute-done((bf16[2,128,256]{2,1,0:T(8,128)(2,1)}, bf16[2,128,256]{2,1,0:T(8,128)(2,1)S(1)}, u32[]{:S(2)}, u32[]{:S(2)}) %collective-permute-start.7) | collective-permute-done | bytes 131104 | tf_op jit(solution)/shard_map/ppermute | solution.py:384
  98.8 1.6 %place.3 = bf16[2,4,512,256]{3,2,1,0:T(8,128)(2,1)} custom-call(s32[9]{0:T(128)S(1)} %concatenate.3.where, bf16[2,2,64,256]{3,2,1,0:T(8,128)(2,1)S(1)} %bitcast.34, bf16[2,2,64,256]{3,2,1,0:T(8,128)(2,1)S(1)} %bitcast.35, bf16[2,2,64,256]{3,2,1,0:T(8,128)(2,1)S(1)} %bitcast.36, bf16[2,2,64,256]{3,2,1,0:T(8,128)(2,1)S(1)} %bitcast.37, ...), custom_call_target="tpu_custom_call", output_to_operand_aliasing={{}: (9, {})} | custom-call | bytes 2097152 | tf_op jit(solution)/shard_map/place/pallas_call | solution.py:288
  (28 shorter events, 0.1 us)
Async XLA Ops:
  1.2 5.4 %copy-start.1 = (bf16[3,3,256,256]{3,2,1,0:T(8,128)(2,1)S(1)}, bf16[3,3,256,256]{3,2,1,0:T(8,128)(2,1)}, u32[]{:S(2)}) copy-start(bf16[3,3,256,256]{3,2,1,0:T(8,128)(2,1)} %param.14) | copy-start | bytes 3538948
  1.3 5.4 %copy-start.8 = (f32[256]{0:T(256)S(1)}, f32[256]{0:T(256)}, u32[]{:S(2)}) copy-start(f32[256]{0:T(256)} %param.13) | copy-start | bytes 3076
  1.3 5.4 %copy-start.9 = (f32[256]{0:T(256)S(1)}, f32[256]{0:T(256)}, u32[]{:S(2)}) copy-start(f32[256]{0:T(256)} %param.15) | copy-start | bytes 3076
  1.3 5.4 %collective-permute-start.1 = (bf16[2,2,512,256]{3,2,1,0:T(8,128)(2,1)S(1)}, bf16[2,2,512,256]{3,2,1,0:T(8,128)(2,1)}, u32[]{:S(2)}, u32[]{:S(2)}) collective-permute-start(bf16[2,2,512,256]{3,2,1,0:T(8,128)(2,1)S(1)} %cut.3.inner), channel_id=1, source_target_pairs={{0,1},{1,0},{2,3},{3,2},{4,5},{5,4},{6,7},{7,6},{8,9},{9,8},{10,11... | collective-permute-start | bytes 3145736 | tf_op jit(solution)/shard_map/ppermute | solution.py:363
  2.7 22.8 %collective-permute-start = (bf16[2,2,512,256]{3,2,1,0:T(8,128)(2,1)S(1)}, bf16[2,2,512,256]{3,2,1,0:T(8,128)(2,1)}, u32[]{:S(2)}, u32[]{:S(2)}) collective-permute-start(bf16[2,2,512,256]{3,2,1,0:T(8,128)(2,1)S(1)} %cut.2.outer), channel_id=1, source_target_pairs={{1,2},{2,1},{3,4},{4,3},{5,6},{6,5},{7,8},{8,7},{9,10},{10,9},{11,... | collective-permute-start | bytes 3145736 | tf_op jit(solution)/shard_map/ppermute | solution.py:361
  6.7 1.3 %copy-start.2 = (bf16[3,3,256,256]{3,2,1,0:T(8,128)(2,1)S(1)}, bf16[3,3,256,256]{3,2,1,0:T(8,128)(2,1)}, u32[]{:S(2)}) copy-start(bf16[3,3,256,256]{3,2,1,0:T(8,128)(2,1)} %param.16) | copy-start | bytes 3538948
  18.8 25.3 %all-to-all-start.1 = ((bf16[8,2,2,64,256]{4,3,2,1,0:T(8,128)(2,1)}), bf16[8,2,2,64,256]{4,3,2,1,0:T(8,128)(2,1)S(1)}, u32[]{:S(2)}, u32[]{:S(2)}) async-start(bf16[8,2,2,64,256]{4,3,2,1,0:T(8,128)(2,1)} %get-tuple-element.24), calls=%async_computation.1 | async-start | bytes 2097152 | tf_op jit(solution)/shard_map/all_to_all | solution.py:371
  35.0 12.9 %copy-start.3 = (bf16[3,256,256]{2,1,0:T(8,128)(2,1)S(1)}, bf16[3,256,256]{2,1,0:T(8,128)(2,1)}, u32[]{:S(2)}) copy-start(bf16[3,256,256]{2,1,0:T(8,128)(2,1)} %param.18) | copy-start | bytes 1179652
  35.0 12.9 %copy-start.4 = (bf16[256,256]{1,0:T(8,128)(2,1)S(1)}, bf16[256,256]{1,0:T(8,128)(2,1)}, u32[]{:S(2)}) copy-start(bf16[256,256]{1,0:T(8,128)(2,1)} %wq.3) | copy-start | bytes 393220
  35.1 12.9 %copy-start.5 = (bf16[256,256]{1,0:T(8,128)(2,1)S(1)}, bf16[256,256]{1,0:T(8,128)(2,1)}, u32[]{:S(2)}) copy-start(bf16[256,256]{1,0:T(8,128)(2,1)} %wk.3) | copy-start | bytes 393220
  35.1 12.9 %copy-start.6 = (bf16[256,256]{1,0:T(8,128)(2,1)S(1)}, bf16[256,256]{1,0:T(8,128)(2,1)}, u32[]{:S(2)}) copy-start(bf16[256,256]{1,0:T(8,128)(2,1)} %wv.3) | copy-start | bytes 393220
  35.1 12.9 %copy-start.7 = (bf16[256,256]{1,0:T(8,128)(2,1)S(1)}, bf16[256,256]{1,0:T(8,128)(2,1)}, u32[]{:S(2)}) copy-start(bf16[256,256]{1,0:T(8,128)(2,1)} %wo.3) | copy-start | bytes 393220
  35.1 12.9 %copy-start.10 = (f32[256]{0:T(256)S(1)}, f32[256]{0:T(256)}, u32[]{:S(2)}) copy-start(f32[256]{0:T(256)} %param.17) | copy-start | bytes 3076
  35.1 12.9 %copy-start.11 = (f32[256]{0:T(256)S(1)}, f32[256]{0:T(256)}, u32[]{:S(2)}) copy-start(f32[256]{0:T(256)} %param.19) | copy-start | bytes 3076
  44.2 20.1 %all-to-all-start = ((bf16[8,2,2,64,256]{4,3,2,1,0:T(8,128)(2,1)}), bf16[8,2,2,64,256]{4,3,2,1,0:T(8,128)(2,1)S(1)}, u32[]{:S(2)}, u32[]{:S(2)}) async-start(bf16[8,2,2,64,256]{4,3,2,1,0:T(8,128)(2,1)} %convs_outer.1), calls=%async_computation | async-start | bytes 2097152 | tf_op jit(solution)/shard_map/all_to_all | solution.py:371
  64.2 29.4 %all-to-all-start.2 = ((bf16[8,2,2,64,256]{4,3,2,1,0:T(8,128)(2,1)}), bf16[8,2,2,64,256]{4,3,2,1,0:T(8,128)(2,1)S(1)}, u32[]{:S(2)}, u32[]{:S(2)}) async-start(bf16[8,2,2,64,256]{4,3,2,1,0:T(8,128)(2,1)} %bitcast.56), calls=%async_computation.2 | async-start | bytes 2097152 | tf_op jit(solution)/shard_map/all_to_all | solution.py:371
  74.4 24.4 %copy-start = (bf16[2,128,256]{2,1,0:T(8,128)(2,1)S(1)}, bf16[2,128,256]{2,1,0:T(8,128)(2,1)}, u32[]{:S(2)}) copy-start(bf16[2,128,256]{2,1,0:T(8,128)(2,1)} %get-tuple-element.16) | copy-start | bytes 393220
  74.4 16.0 %collective-permute-start.2 = (bf16[2,128,256]{2,1,0:T(8,128)(2,1)}, bf16[2,128,256]{2,1,0:T(8,128)(2,1)S(1)}, u32[]{:S(2)}, u32[]{:S(2)}) collective-permute-start(bf16[2,128,256]{2,1,0:T(8,128)(2,1)} %get-tuple-element.17), channel_id=1, source_target_pairs={{0,160},{32,128},{64,224},{96,192},{128,32},{160,0},{192,96},{224,... | collective-permute-start | bytes 393224 | tf_op jit(solution)/shard_map/ppermute | solution.py:384
  80.3 12.7 %collective-permute-start.3 = (bf16[2,128,256]{2,1,0:T(8,128)(2,1)}, bf16[2,128,256]{2,1,0:T(8,128)(2,1)S(1)}, u32[]{:S(2)}, u32[]{:S(2)}) collective-permute-start(bf16[2,128,256]{2,1,0:T(8,128)(2,1)} %get-tuple-element.18), channel_id=1, source_target_pairs={{0,96},{32,64},{64,160},{96,128},{128,224},{160,192},{192,32},{224... | collective-permute-start | bytes 393224 | tf_op jit(solution)/shard_map/ppermute | solution.py:384
  80.9 14.4 %collective-permute-start.4 = (bf16[2,128,256]{2,1,0:T(8,128)(2,1)}, bf16[2,128,256]{2,1,0:T(8,128)(2,1)S(1)}, u32[]{:S(2)}, u32[]{:S(2)}) collective-permute-start(bf16[2,128,256]{2,1,0:T(8,128)(2,1)} %get-tuple-element.19), channel_id=1, source_target_pairs={{0,224},{32,192},{64,32},{96,0},{128,96},{160,64},{192,160},{224,1... | collective-permute-start | bytes 393224 | tf_op jit(solution)/shard_map/ppermute | solution.py:384
  85.9 10.1 %collective-permute-start.5 = (bf16[2,128,256]{2,1,0:T(8,128)(2,1)}, bf16[2,128,256]{2,1,0:T(8,128)(2,1)S(1)}, u32[]{:S(2)}, u32[]{:S(2)}) collective-permute-start(bf16[2,128,256]{2,1,0:T(8,128)(2,1)} %get-tuple-element.20), channel_id=1, source_target_pairs={{0,128},{32,160},{64,192},{96,224},{128,0},{160,32},{192,64},{224,... | collective-permute-start | bytes 393224 | tf_op jit(solution)/shard_map/ppermute | solution.py:384
  85.9 10.4 %collective-permute-start.6 = (bf16[2,128,256]{2,1,0:T(8,128)(2,1)}, bf16[2,128,256]{2,1,0:T(8,128)(2,1)S(1)}, u32[]{:S(2)}, u32[]{:S(2)}) collective-permute-start(bf16[2,128,256]{2,1,0:T(8,128)(2,1)} %get-tuple-element.21), channel_id=1, source_target_pairs={{0,32},{32,0},{64,96},{96,64},{128,160},{160,128},{192,224},{224,1... | collective-permute-start | bytes 393224 | tf_op jit(solution)/shard_map/ppermute | solution.py:384
  90.4 8.4 %collective-permute-start.7 = (bf16[2,128,256]{2,1,0:T(8,128)(2,1)}, bf16[2,128,256]{2,1,0:T(8,128)(2,1)S(1)}, u32[]{:S(2)}, u32[]{:S(2)}) collective-permute-start(bf16[2,128,256]{2,1,0:T(8,128)(2,1)} %get-tuple-element.22), channel_id=1, source_target_pairs={{0,64},{32,96},{64,128},{96,160},{128,192},{160,224},{192,0},{224,... | collective-permute-start | bytes 393224 | tf_op jit(solution)/shard_map/ppermute | solution.py:384
  93.0 5.9 %collective-permute-start.8 = (bf16[2,128,256]{2,1,0:T(8,128)(2,1)}, bf16[2,128,256]{2,1,0:T(8,128)(2,1)S(1)}, u32[]{:S(2)}, u32[]{:S(2)}) collective-permute-start(bf16[2,128,256]{2,1,0:T(8,128)(2,1)} %get-tuple-element.23), channel_id=1, source_target_pairs={{0,192},{32,224},{64,0},{96,32},{128,64},{160,96},{192,128},{224,1... | collective-permute-start | bytes 393224 | tf_op jit(solution)/shard_map/ppermute | solution.py:384

commit v5 on v4

--- a/solution.py
+++ b/solution.py
@@ -47,12 +47,14 @@
     return copy
 
 
-def inner_body(info, inner, outer, halo, gain_one, w_one, gain_two, w_two,
-               out, shared, s_one, s_two, kept, held, kept_sems, sems):
+def inner_body(info, inner, outer, halo, gain_one, w_one, gain_two, conv_two,
+               out, shared, s_one, s_two, kept, w_two, held, kept_sems, w_sem, sems):
     frames, _, width, chans = inner.shape
     odd = info[0] == 1
     half_one = gain_one[...] * 0.5
     half_two = gain_two[...] * 0.5
+    load = pltpu.make_async_copy(conv_two, w_two, w_sem)
+    load.start()
 
     def put_first(frame, index):
         if index < HALF:
@@ -69,6 +71,7 @@
 
     for index in range(3 * HALF):
         put_first(0, index)
+    load.wait()
     copies = []
     for frame in range(frames):
         for index in range(2 * HALF):
@@ -162,7 +165,7 @@
         outer_body if is_outer else inner_body,
         in_specs=[
             pl.BlockSpec(memory_space=pltpu.SMEM), here, here, there if is_outer else here,
-            here, here, here, there if is_outer else here,
+            here, here, here, there,
         ],
         out_specs=[there] if is_outer else [there, there],
         out_shape=[mixed] if is_outer else [mixed, keep],
@@ -170,10 +173,10 @@
             stack(first_rows),
             *two,
             pltpu.VMEM((frames, HALF, cols, chans), BF16),
-            *([pltpu.VMEM(conv_two.shape, BF16)] if is_outer else []),
+            pltpu.VMEM(conv_two.shape, BF16),
             pltpu.VMEM((frames, HALF, owners, own, chans), BF16),
             pltpu.SemaphoreType.DMA((frames,)),
-            *([pltpu.SemaphoreType.DMA] if is_outer else []),
+            pltpu.SemaphoreType.DMA,
             pltpu.SemaphoreType.DMA((frames, HALF)),
         ],
         compiler_params=pltpu.CompilerParams(vmem_limit_bytes=28 * 1024 * 1024),
@@ -183,7 +186,7 @@
         name="convs_outer" if is_outer else "convs_inner",
     )(
         info, *((outer, halo, far(shared)) if is_outer else (inner, outer, halo)),
-        gain_one, near(conv_one), gain_two, far(conv_two) if is_outer else near(conv_two),
+        gain_one, near(conv_one), gain_two, far(conv_two),
     )
 
 

time: 101 us -> 100 us (0.990)
  waiting for transfers between devices: 29.3 us -> 27.6 us
  local copies, waits for them, and re-layouts: 1.51 us -> 0.24 us
    unnamed x24 -> x22, local copies, waits for them, and re-layouts: 1.33 us -> 0.07 us
  transfers between devices with their start and end apart: 12 -> 12, of which waited for: 7 -> 6; matrix products, arithmetic and copies ran while one was open for 0% -> 0% of each run, Pallas kernels for 35% -> 37%
where the time goes in v5:
time: 100 us; the launch traced here: 98.9 us
  Pallas kernels  39 us (39%)
  starting transfers between devices  31.5 us (32%)
  waiting for transfers between devices  27.6 us (28%)
    pallas_call x2, Pallas kernels, conv_chunk(): pl.pallas_call(outer_body if is_outer else inner_body, in_specs=[pl.Block...  21.2 us
    all_to_all x3, waiting for transfers between devices, shards(): lax.all_to_all(v, 'tm', split_axis=0, concat_axis=0, tiled=True)  18.5 us
    all_to_all x3, starting transfers between devices, shards(): lax.all_to_all(v, 'tm', split_axis=0, concat_axis=0, tiled=True)  14.3 us
    ppermute x7, starting transfers between devices, shards(): lax.ppermute(finals[n], 'tm', [(i, member(i, dy, dx)) for i in range(owne...  13.2 us
    pallas_call x2, Pallas kernels, attend_chunk(): pl.pallas_call(functools.partial(attend_body, group), grid=(pixels // til...  12 us
    ppermute x7, waiting for transfers between devices, shards(): lax.ppermute(finals[n], 'tm', [(i, member(i, dy, dx)) for i in range(owne...  9.1 us
    ppermute x1, starting transfers between devices, shards(): from_outer = lax.ppermute(outer, 'strip', neighbours)  3.87 us
    pallas_call x2, Pallas kernels, place(): pl.pallas_call(functools.partial(place_body, len(pieces)), in_specs=[scal...  3.16 us
  transfers between devices with their start and end apart: 12, of which 6 were waited for; matrix products, arithmetic and copies ran while one was open for 0% of the time, Pallas kernels for 37%

profile of v5, /device:TPU:160, one launch (start us, length us, event | category | flops | bytes accessed | tf_op | source)
XLA Modules:
  0.0 98.9 jit_solution(14966807451551574992)
XLA Ops:
  0.0 1.2 %cut.3.inner = bf16[2,2,512,256]{3,2,1,0:T(8,128)(2,1)S(1)} custom-call(s32[1]{0:T(128)} %bitcast.13.start, bf16[2,4,512,256]{3,2,1,0:T(8,128)(2,1)} %video.3), custom_call_target="tpu_custom_call" | custom-call | bytes 2097152 | tf_op jit(solution)/shard_map/cut/pallas_call | solution.py:314
  1.3 0.0 copy-start.8
  1.3 0.1 collective-permute-start.1
  1.4 1.3 %cut.2.outer = bf16[2,2,512,256]{3,2,1,0:T(8,128)(2,1)S(1)} custom-call(s32[1]{0:T(128)} %bitcast.start, bf16[2,4,512,256]{3,2,1,0:T(8,128)(2,1)} %video.3), custom_call_target="tpu_custom_call" | custom-call | bytes 2097152 | tf_op jit(solution)/shard_map/cut/pallas_call | solution.py:314
  2.7 3.9 %collective-permute-start = (bf16[2,2,512,256]{3,2,1,0:T(8,128)(2,1)S(1)}, bf16[2,2,512,256]{3,2,1,0:T(8,128)(2,1)}, u32[]{:S(2)}, u32[]{:S(2)}) collective-permute-start(bf16[2,2,512,256]{3,2,1,0:T(8,128)(2,1)S(1)} %cut.2.outer), channel_id=1, source_target_pairs={{1,2},{2,1},{3,4},{4,3},{5,6},{6,5},{7,8},{8,7},{9,10},{10,9},{11,... | collective-permute-start | bytes 3145736 | tf_op jit(solution)/shard_map/ppermute | solution.py:364
  6.6 0.1 pad_add_fusion.info
  6.7 11.7 %convs_inner.1 = (bf16[8,2,2,64,256]{4,3,2,1,0:T(8,128)(2,1)}, bf16[2,2,512,256]{3,2,1,0:T(8,128)(2,1)}) custom-call(s32[2]{0:T(128)S(1)} %pad_add_fusion.info, bf16[2,2,512,256]{3,2,1,0:T(8,128)(2,1)S(1)} %cut.3.inner, bf16[2,2,512,256]{3,2,1,0:T(8,128)(2,1)S(1)} %cut.2.outer, bf16[2,2,512,256]{3,2,1,0:T(8,128)(2,1)} %collective-permute-done.1.halo, ...), custom_call_target="tpu_custom_call" | custom-call | flops 7247757312 | bytes 8388608 | tf_op jit(solution)/shard_map/convs_inner/pallas_call | solution.py:164
  18.4 6.6 %all-to-all-start.1 = ((bf16[8,2,2,64,256]{4,3,2,1,0:T(8,128)(2,1)}), bf16[8,2,2,64,256]{4,3,2,1,0:T(8,128)(2,1)S(1)}, u32[]{:S(2)}, u32[]{:S(2)}) async-start(bf16[8,2,2,64,256]{4,3,2,1,0:T(8,128)(2,1)} %get-tuple-element.24), calls=%async_computation.1 | async-start | bytes 2097152 | tf_op jit(solution)/shard_map/all_to_all | solution.py:374
  25.1 9.5 %convs_outer.1 = bf16[8,2,2,64,256]{4,3,2,1,0:T(8,128)(2,1)} custom-call(s32[2]{0:T(128)S(1)} %pad_add_fusion.info, bf16[2,2,512,256]{3,2,1,0:T(8,128)(2,1)S(1)} %cut.2.outer, bf16[2,2,512,256]{3,2,1,0:T(8,128)(2,1)} %collective-permute-done.halo, bf16[2,2,512,256]{3,2,1,0:T(8,128)(2,1)} %get-tuple-element.15.shared, f32[1,256]{1,0:T(1,128)S(1)} %bitcast.47, ...), custom_call_target="tpu_custom_call" | custom-call | flops 4831838208 | bytes 8388608 | tf_op jit(solution)/shard_map/convs_outer/pallas_call | solution.py:164
  34.6 0.0 copy-start.2
  34.6 0.0 copy-start.3
  34.6 0.0 copy-start.6
  34.7 9.1 %all-to-all-done.1 = bf16[8,2,2,64,256]{4,3,2,1,0:T(8,128)(2,1)S(1)} async-done(((bf16[8,2,2,64,256]{4,3,2,1,0:T(8,128)(2,1)}), bf16[8,2,2,64,256]{4,3,2,1,0:T(8,128)(2,1)S(1)}, u32[]{:S(2)}, u32[]{:S(2)}) %all-to-all-start.1) | async-done | bytes 1048608 | tf_op jit(solution)/shard_map/all_to_all | solution.py:374
  43.7 3.6 %all-to-all-start = ((bf16[8,2,2,64,256]{4,3,2,1,0:T(8,128)(2,1)}), bf16[8,2,2,64,256]{4,3,2,1,0:T(8,128)(2,1)S(1)}, u32[]{:S(2)}, u32[]{:S(2)}) async-start(bf16[8,2,2,64,256]{4,3,2,1,0:T(8,128)(2,1)} %convs_outer.1), calls=%async_computation | async-start | bytes 2097152 | tf_op jit(solution)/shard_map/all_to_all | solution.py:374
  47.4 0.1 stack.68.order
  47.6 6.0 %attend.3 = bf16[16,128,256]{2,1,0:T(8,128)(2,1)} custom-call(s32[8]{0:T(128)S(1)} %stack.68.order, bf16[16,128,256]{2,1,0:T(8,128)(2,1)S(1)} %bitcast.33, f32[1,256]{1,0:T(1,128)S(1)} %bitcast.50, bf16[768,256]{1,0:T(8,128)(2,1)S(1)} %bitcast.44, f32[1,256]{1,0:T(1,128)S(1)} %bitcast.52, bf16[256,256]{1,0:T(8,128)(2,1)S(1)} %copy-done.3, ...), custom_call_target="tpu_custom_call" | custom-call | flops 2415919104 | bytes 4194304 | tf_op jit(solution)/shard_map/attend/pallas_call | solution.py:248
  53.6 9.4 %all-to-all-done = bf16[8,2,2,64,256]{4,3,2,1,0:T(8,128)(2,1)S(1)} async-done(((bf16[8,2,2,64,256]{4,3,2,1,0:T(8,128)(2,1)}), bf16[8,2,2,64,256]{4,3,2,1,0:T(8,128)(2,1)S(1)}, u32[]{:S(2)}, u32[]{:S(2)}) %all-to-all-start) | async-done | bytes 1048608 | tf_op jit(solution)/shard_map/all_to_all | solution.py:374
  63.0 4.1 %all-to-all-start.2 = ((bf16[8,2,2,64,256]{4,3,2,1,0:T(8,128)(2,1)}), bf16[8,2,2,64,256]{4,3,2,1,0:T(8,128)(2,1)S(1)}, u32[]{:S(2)}, u32[]{:S(2)}) async-start(bf16[8,2,2,64,256]{4,3,2,1,0:T(8,128)(2,1)} %bitcast.54), calls=%async_computation.2 | async-start | bytes 2097152 | tf_op jit(solution)/shard_map/all_to_all | solution.py:374
  67.1 6.0 %attend.2 = (bf16[2,128,256]{2,1,0:T(8,128)(2,1)}, bf16[2,128,256]{2,1,0:T(8,128)(2,1)}, bf16[2,128,256]{2,1,0:T(8,128)(2,1)}, bf16[2,128,256]{2,1,0:T(8,128)(2,...) custom-call(s32[8]{0:T(128)S(1)} %stack.68.order, ...), custom_call_target="tpu_custom_call" | custom-call | flops 2415919104 | bytes 4194304 | tf_op jit(solution)/shard_map/attend/pallas_call | solution.py:248
  73.1 5.9 %collective-permute-start.2 = (bf16[2,128,256]{2,1,0:T(8,128)(2,1)}, bf16[2,128,256]{2,1,0:T(8,128)(2,1)S(1)}, u32[]{:S(2)}, u32[]{:S(2)}) collective-permute-start(bf16[2,128,256]{2,1,0:T(8,128)(2,1)} %get-tuple-element.17), channel_id=1, source_target_pairs={{0,160},{32,128},{64,224},{96,192},{128,32},{160,0},{192,96},{224,... | collective-permute-start | bytes 393224 | tf_op jit(solution)/shard_map/ppermute | solution.py:387
  79.1 0.6 collective-permute-start.3
  79.6 5.1 %collective-permute-start.4 = (bf16[2,128,256]{2,1,0:T(8,128)(2,1)}, bf16[2,128,256]{2,1,0:T(8,128)(2,1)S(1)}, u32[]{:S(2)}, u32[]{:S(2)}) collective-permute-start(bf16[2,128,256]{2,1,0:T(8,128)(2,1)} %get-tuple-element.19), channel_id=1, source_target_pairs={{0,224},{32,192},{64,32},{96,0},{128,96},{160,64},{192,160},{224,1... | collective-permute-start | bytes 393224 | tf_op jit(solution)/shard_map/ppermute | solution.py:387
  84.7 0.6 collective-permute-start.6
  85.3 2.6 %collective-permute-done.2 = bf16[2,128,256]{2,1,0:T(8,128)(2,1)S(1)} collective-permute-done((bf16[2,128,256]{2,1,0:T(8,128)(2,1)}, bf16[2,128,256]{2,1,0:T(8,128)(2,1)S(1)}, u32[]{:S(2)}, u32[]{:S(2)}) %collective-permute-start.2) | collective-permute-done | bytes 131104 | tf_op jit(solution)/shard_map/ppermute | solution.py:387
  87.8 0.4 collective-permute-start.7
  88.3 2.2 %collective-permute-done.3 = bf16[2,128,256]{2,1,0:T(8,128)(2,1)S(1)} collective-permute-done((bf16[2,128,256]{2,1,0:T(8,128)(2,1)}, bf16[2,128,256]{2,1,0:T(8,128)(2,1)S(1)}, u32[]{:S(2)}, u32[]{:S(2)}) %collective-permute-start.3) | collective-permute-done | bytes 131104 | tf_op jit(solution)/shard_map/ppermute | solution.py:387
  90.5 0.6 collective-permute-start.8
  91.1 0.1 concatenate.3.where
  91.2 1.6 %place.2.refs_8_ = bf16[2,4,512,256]{3,2,1,0:T(8,128)(2,1)} custom-call(s32[9]{0:T(128)S(1)} %broadcast_in_dim.2.where, bf16[8,2,2,64,256]{4,3,2,1,0:T(8,128)(2,1)S(1)} %all-to-all-done.2.refs_0_), custom_call_target="tpu_custom_call" | custom-call | bytes 2097152 | tf_op jit(solution)/shard_map/place/pallas_call | solution.py:291
  92.8 1.7 %collective-permute-done.5 = bf16[2,128,256]{2,1,0:T(8,128)(2,1)S(1)} collective-permute-done((bf16[2,128,256]{2,1,0:T(8,128)(2,1)}, bf16[2,128,256]{2,1,0:T(8,128)(2,1)S(1)}, u32[]{:S(2)}, u32[]{:S(2)}) %collective-permute-start.5) | collective-permute-done | bytes 131104 | tf_op jit(solution)/shard_map/ppermute | solution.py:387
  94.5 2.6 %collective-permute-done.7 = bf16[2,128,256]{2,1,0:T(8,128)(2,1)S(1)} collective-permute-done((bf16[2,128,256]{2,1,0:T(8,128)(2,1)}, bf16[2,128,256]{2,1,0:T(8,128)(2,1)S(1)}, u32[]{:S(2)}, u32[]{:S(2)}) %collective-permute-start.7) | collective-permute-done | bytes 131104 | tf_op jit(solution)/shard_map/ppermute | solution.py:387
  97.2 1.6 %place.3 = bf16[2,4,512,256]{3,2,1,0:T(8,128)(2,1)} custom-call(s32[9]{0:T(128)S(1)} %concatenate.3.where, bf16[2,2,64,256]{3,2,1,0:T(8,128)(2,1)S(1)} %bitcast.34, bf16[2,2,64,256]{3,2,1,0:T(8,128)(2,1)S(1)} %bitcast.35, bf16[2,2,64,256]{3,2,1,0:T(8,128)(2,1)S(1)} %bitcast.36, bf16[2,2,64,256]{3,2,1,0:T(8,128)(2,1)S(1)} %bitcast.37, ...), custom_call_target="tpu_custom_call", output_to_operand_aliasing={{}: (9, {})} | custom-call | bytes 2097152 | tf_op jit(solution)/shard_map/place/pallas_call | solution.py:291
  (26 shorter events, 0.1 us)
Async XLA Ops:
  1.2 5.4 %copy-start.1 = (bf16[3,3,256,256]{3,2,1,0:T(8,128)(2,1)S(1)}, bf16[3,3,256,256]{3,2,1,0:T(8,128)(2,1)}, u32[]{:S(2)}) copy-start(bf16[3,3,256,256]{3,2,1,0:T(8,128)(2,1)} %param.14) | copy-start | bytes 3538948
  1.3 5.4 %copy-start.7 = (f32[256]{0:T(256)S(1)}, f32[256]{0:T(256)}, u32[]{:S(2)}) copy-start(f32[256]{0:T(256)} %param.13) | copy-start | bytes 3076
  1.3 5.4 %copy-start.8 = (f32[256]{0:T(256)S(1)}, f32[256]{0:T(256)}, u32[]{:S(2)}) copy-start(f32[256]{0:T(256)} %param.15) | copy-start | bytes 3076
  1.3 5.4 %collective-permute-start.1 = (bf16[2,2,512,256]{3,2,1,0:T(8,128)(2,1)S(1)}, bf16[2,2,512,256]{3,2,1,0:T(8,128)(2,1)}, u32[]{:S(2)}, u32[]{:S(2)}) collective-permute-start(bf16[2,2,512,256]{3,2,1,0:T(8,128)(2,1)S(1)} %cut.3.inner), channel_id=1, source_target_pairs={{0,1},{1,0},{2,3},{3,2},{4,5},{5,4},{6,7},{7,6},{8,9},{9,8},{10,11... | collective-permute-start | bytes 3145736 | tf_op jit(solution)/shard_map/ppermute | solution.py:366
  2.7 22.4 %collective-permute-start = (bf16[2,2,512,256]{3,2,1,0:T(8,128)(2,1)S(1)}, bf16[2,2,512,256]{3,2,1,0:T(8,128)(2,1)}, u32[]{:S(2)}, u32[]{:S(2)}) collective-permute-start(bf16[2,2,512,256]{3,2,1,0:T(8,128)(2,1)S(1)} %cut.2.outer), channel_id=1, source_target_pairs={{1,2},{2,1},{3,4},{4,3},{5,6},{6,5},{7,8},{8,7},{9,10},{10,9},{11,... | collective-permute-start | bytes 3145736 | tf_op jit(solution)/shard_map/ppermute | solution.py:364
  18.4 25.3 %all-to-all-start.1 = ((bf16[8,2,2,64,256]{4,3,2,1,0:T(8,128)(2,1)}), bf16[8,2,2,64,256]{4,3,2,1,0:T(8,128)(2,1)S(1)}, u32[]{:S(2)}, u32[]{:S(2)}) async-start(bf16[8,2,2,64,256]{4,3,2,1,0:T(8,128)(2,1)} %get-tuple-element.24), calls=%async_computation.1 | async-start | bytes 2097152 | tf_op jit(solution)/shard_map/all_to_all | solution.py:374
  34.6 12.9 %copy-start.2 = (bf16[3,256,256]{2,1,0:T(8,128)(2,1)S(1)}, bf16[3,256,256]{2,1,0:T(8,128)(2,1)}, u32[]{:S(2)}) copy-start(bf16[3,256,256]{2,1,0:T(8,128)(2,1)} %param.18) | copy-start | bytes 1179652
  34.6 12.9 %copy-start.3 = (bf16[256,256]{1,0:T(8,128)(2,1)S(1)}, bf16[256,256]{1,0:T(8,128)(2,1)}, u32[]{:S(2)}) copy-start(bf16[256,256]{1,0:T(8,128)(2,1)} %wq.3) | copy-start | bytes 393220
  34.6 12.9 %copy-start.4 = (bf16[256,256]{1,0:T(8,128)(2,1)S(1)}, bf16[256,256]{1,0:T(8,128)(2,1)}, u32[]{:S(2)}) copy-start(bf16[256,256]{1,0:T(8,128)(2,1)} %wk.3) | copy-start | bytes 393220
  34.6 12.9 %copy-start.5 = (bf16[256,256]{1,0:T(8,128)(2,1)S(1)}, bf16[256,256]{1,0:T(8,128)(2,1)}, u32[]{:S(2)}) copy-start(bf16[256,256]{1,0:T(8,128)(2,1)} %wv.3) | copy-start | bytes 393220
  34.6 12.9 %copy-start.6 = (bf16[256,256]{1,0:T(8,128)(2,1)S(1)}, bf16[256,256]{1,0:T(8,128)(2,1)}, u32[]{:S(2)}) copy-start(bf16[256,256]{1,0:T(8,128)(2,1)} %wo.3) | copy-start | bytes 393220
  34.7 12.9 %copy-start.9 = (f32[256]{0:T(256)S(1)}, f32[256]{0:T(256)}, u32[]{:S(2)}) copy-start(f32[256]{0:T(256)} %param.17) | copy-start | bytes 3076
  34.7 12.9 %copy-start.10 = (f32[256]{0:T(256)S(1)}, f32[256]{0:T(256)}, u32[]{:S(2)}) copy-start(f32[256]{0:T(256)} %param.19) | copy-start | bytes 3076
  43.7 19.2 %all-to-all-start = ((bf16[8,2,2,64,256]{4,3,2,1,0:T(8,128)(2,1)}), bf16[8,2,2,64,256]{4,3,2,1,0:T(8,128)(2,1)S(1)}, u32[]{:S(2)}, u32[]{:S(2)}) async-start(bf16[8,2,2,64,256]{4,3,2,1,0:T(8,128)(2,1)} %convs_outer.1), calls=%async_computation | async-start | bytes 2097152 | tf_op jit(solution)/shard_map/all_to_all | solution.py:374
  63.0 28.2 %all-to-all-start.2 = ((bf16[8,2,2,64,256]{4,3,2,1,0:T(8,128)(2,1)}), bf16[8,2,2,64,256]{4,3,2,1,0:T(8,128)(2,1)S(1)}, u32[]{:S(2)}, u32[]{:S(2)}) async-start(bf16[8,2,2,64,256]{4,3,2,1,0:T(8,128)(2,1)} %bitcast.54), calls=%async_computation.2 | async-start | bytes 2097152 | tf_op jit(solution)/shard_map/all_to_all | solution.py:374
  73.1 24.0 %copy-start = (bf16[2,128,256]{2,1,0:T(8,128)(2,1)S(1)}, bf16[2,128,256]{2,1,0:T(8,128)(2,1)}, u32[]{:S(2)}) copy-start(bf16[2,128,256]{2,1,0:T(8,128)(2,1)} %get-tuple-element.16) | copy-start | bytes 393220
  73.1 14.7 %collective-permute-start.2 = (bf16[2,128,256]{2,1,0:T(8,128)(2,1)}, bf16[2,128,256]{2,1,0:T(8,128)(2,1)S(1)}, u32[]{:S(2)}, u32[]{:S(2)}) collective-permute-start(bf16[2,128,256]{2,1,0:T(8,128)(2,1)} %get-tuple-element.17), channel_id=1, source_target_pairs={{0,160},{32,128},{64,224},{96,192},{128,32},{160,0},{192,96},{224,... | collective-permute-start | bytes 393224 | tf_op jit(solution)/shard_map/ppermute | solution.py:387
  79.1 11.4 %collective-permute-start.3 = (bf16[2,128,256]{2,1,0:T(8,128)(2,1)}, bf16[2,128,256]{2,1,0:T(8,128)(2,1)S(1)}, u32[]{:S(2)}, u32[]{:S(2)}) collective-permute-start(bf16[2,128,256]{2,1,0:T(8,128)(2,1)} %get-tuple-element.18), channel_id=1, source_target_pairs={{0,96},{32,64},{64,160},{96,128},{128,224},{160,192},{192,32},{224... | collective-permute-start | bytes 393224 | tf_op jit(solution)/shard_map/ppermute | solution.py:387
  79.6 13.2 %collective-permute-start.4 = (bf16[2,128,256]{2,1,0:T(8,128)(2,1)}, bf16[2,128,256]{2,1,0:T(8,128)(2,1)S(1)}, u32[]{:S(2)}, u32[]{:S(2)}) collective-permute-start(bf16[2,128,256]{2,1,0:T(8,128)(2,1)} %get-tuple-element.19), channel_id=1, source_target_pairs={{0,224},{32,192},{64,32},{96,0},{128,96},{160,64},{192,160},{224,1... | collective-permute-start | bytes 393224 | tf_op jit(solution)/shard_map/ppermute | solution.py:387
  84.7 9.8 %collective-permute-start.5 = (bf16[2,128,256]{2,1,0:T(8,128)(2,1)}, bf16[2,128,256]{2,1,0:T(8,128)(2,1)S(1)}, u32[]{:S(2)}, u32[]{:S(2)}) collective-permute-start(bf16[2,128,256]{2,1,0:T(8,128)(2,1)} %get-tuple-element.20), channel_id=1, source_target_pairs={{0,128},{32,160},{64,192},{96,224},{128,0},{160,32},{192,64},{224,... | collective-permute-start | bytes 393224 | tf_op jit(solution)/shard_map/ppermute | solution.py:387
  84.7 9.8 %collective-permute-start.6 = (bf16[2,128,256]{2,1,0:T(8,128)(2,1)}, bf16[2,128,256]{2,1,0:T(8,128)(2,1)S(1)}, u32[]{:S(2)}, u32[]{:S(2)}) collective-permute-start(bf16[2,128,256]{2,1,0:T(8,128)(2,1)} %get-tuple-element.21), channel_id=1, source_target_pairs={{0,32},{32,0},{64,96},{96,64},{128,160},{160,128},{192,224},{224,1... | collective-permute-start | bytes 393224 | tf_op jit(solution)/shard_map/ppermute | solution.py:387
  87.8 9.3 %collective-permute-start.7 = (bf16[2,128,256]{2,1,0:T(8,128)(2,1)}, bf16[2,128,256]{2,1,0:T(8,128)(2,1)S(1)}, u32[]{:S(2)}, u32[]{:S(2)}) collective-permute-start(bf16[2,128,256]{2,1,0:T(8,128)(2,1)} %get-tuple-element.22), channel_id=1, source_target_pairs={{0,64},{32,96},{64,128},{96,160},{128,192},{160,224},{192,0},{224,... | collective-permute-start | bytes 393224 | tf_op jit(solution)/shard_map/ppermute | solution.py:387
  90.5 6.6 %collective-permute-start.8 = (bf16[2,128,256]{2,1,0:T(8,128)(2,1)}, bf16[2,128,256]{2,1,0:T(8,128)(2,1)S(1)}, u32[]{:S(2)}, u32[]{:S(2)}) collective-permute-start(bf16[2,128,256]{2,1,0:T(8,128)(2,1)} %get-tuple-element.23), channel_id=1, source_target_pairs={{0,192},{32,224},{64,0},{96,32},{128,64},{160,96},{192,128},{224,1... | collective-permute-start | bytes 393224 | tf_op jit(solution)/shard_map/ppermute | solution.py:387
